TPU v7x, 32 devices: a whole 2x2x4 slice. The times are simulated.
32 devices in a mesh: gx: 4 (over x, core), gy: 2 (over y), gz: 4 (over z).
Axes of the slice: x: 2, y: 2, z: 4, core: 2. Of those that a mesh axis runs over, the one named last changes fastest.
Arguments:
- phase: int32 [256, 16, 512], P('gx', 'gy', 'gz'), may hold values from 0 to 2
- perm_scale: float32 [256, 16, 512], P('gx', 'gy', 'gz'), may hold values from 0.5 to 2
- magnetization: bfloat16 [3, 256, 16, 512], P(None, 'gx', 'gy', 'gz'), may hold values from -4 to 4
- stiffness: float32 [256, 16, 512], P(('gx', 'gy'), None, 'gz'), may hold values from 0.5 to 4
Outputs:
- strain: bfloat16 [6, 256, 16, 512], P(None, 'gx', 'gy', 'gz')
All inputs are finite; a program needn't handle non-finite values.
Results may differ from a plain program's by a relative error of at most 0.001.
The roundings to bfloat16 on the way count: a program that leaves them out, or rounds other values in their place, can miss the bound.
Values may be sent and summed in bfloat16 or wider, within the bound.
A program may use at most 64 MiB of HBM per device.

v0:
```python
import math

import jax
import jax.numpy as jnp
from jax import lax
from jax.sharding import PartitionSpec as P

SWEEPS = 3


STRAIN_PAIRS = ((0, 0), (1, 1), (2, 2), (0, 1), (1, 2), (0, 2))
MAGNETO = 4.0


def padded_2(value, sides, width):
    for axis, dim in sides:
        devices, length = (lax.axis_size(axis), value.shape[dim])
        up = [(i, (i + 1) % devices) for i in range(devices - 1)]
        down = [(j, i) for i, j in up]
        last = lax.slice_in_dim(value, length - width, length, axis=dim)
        leading = lax.slice_in_dim(value, 0, width, axis=dim)
        before = lax.ppermute(last, axis, up)
        after = lax.ppermute(leading, axis, down)
        value = jnp.concatenate([before, value, after], axis=dim)
    return value


def chebyshev_weights(middle, radius, count):
    return [
        1.0 / (middle + radius * math.cos((2 * counter + 1) * math.pi / (2 * count)))
        for counter in range(count)
    ]


def unit_offset(dimension, sign):
    offsets = [0, 0, 0]
    offsets[dimension] = sign
    return offsets


def window(padded, offsets):
    shape = padded.shape[-3:]
    selection = tuple(
        (slice(1 + moved, extent - 1 + moved) for moved, extent in zip(offsets, shape))
    )
    leading = tuple((slice(None) for counter in range(padded.ndim - 3)))
    return padded[leading + selection]


def central(padded, dimension):
    return (
        window(padded, unit_offset(dimension, 1)) - window(padded, unit_offset(dimension, -1))
    ) * 0.5


def neighbours(padded):
    total = window(padded, unit_offset(0, 1)) + window(padded, unit_offset(0, -1))
    for dimension in (1, 2):
        total = (
            total
            + window(padded, unit_offset(dimension, 1))
            + window(padded, unit_offset(dimension, -1))
        )
    return total


def magnet_force(moments_pad, potential_pad):
    total = [moments_pad[dimension] - central(potential_pad, dimension) for dimension in range(3)]
    inner = moments_pad[0] * total[0] + moments_pad[1] * total[1] + moments_pad[2] * total[2]
    stress = {}
    for first, second in STRAIN_PAIRS:
        value = 0.5 * (moments_pad[first] * total[second] + moments_pad[second] * total[first])
        if first == second:
            value = value - inner / 3.0
        stress[first, second] = MAGNETO * value
        stress[second, first] = stress[first, second]
    force = []
    for first in range(3):
        acc = central(stress[first, 0], 0)
        for second in (1, 2):
            acc = acc + central(stress[first, second], second)
        force.append(acc)
    return jnp.stack(force)


def navier(padded):
    result = []
    for first in range(3):
        center = window(padded[first], [0, 0, 0])
        value = 6.0 * center - neighbours(padded[first])
        second_diff = (
            window(padded[first], unit_offset(first, 1))
            - 2.0 * center
            + window(padded[first], unit_offset(first, -1))
        )
        for second in range(3):
            if second != first:
                plus_plus = [0, 0, 0]
                plus_plus[first] = 1
                plus_plus[second] = 1
                plus_minus = [0, 0, 0]
                plus_minus[first] = 1
                plus_minus[second] = -1
                minus_plus = [0, 0, 0]
                minus_plus[first] = -1
                minus_plus[second] = 1
                minus_minus = [0, 0, 0]
                minus_minus[first] = -1
                minus_minus[second] = -1
                second_diff = second_diff + 0.25 * (
                    window(padded[second], plus_plus)
                    - window(padded[second], plus_minus)
                    - window(padded[second], minus_plus)
                    + window(padded[second], minus_minus)
                )
        result.append(value - second_diff)
    return jnp.stack(result)


def strain_from(padded):
    result = []
    for first, second in STRAIN_PAIRS:
        result.append(0.5 * (central(padded[second], first) + central(padded[first], second)))
    return jnp.stack(result)


def potential_rim(field):
    return padded_2(field, (("gx", 0), ("gy", 1), ("gz", 2)), 2)


def elastic_solve(load, modulus, pad_field):
    elastic_weights = chebyshev_weights(1.3, 1.2, SWEEPS)
    elastic_diag = 8.0 * modulus
    displacement = elastic_weights[0] * load / elastic_diag
    for counter in range(1, SWEEPS):
        padded = pad_field(displacement)
        displacement = (
            displacement
            + elastic_weights[counter] * (load - modulus * navier(padded)) / elastic_diag
        )
    return displacement


def per_device(phase, perm_scale, magnetization, stiffness):
    magnetic = phase == 0
    permeability = (
        jnp.where(magnetic, 4.0, jnp.where(phase == 1, 1.5, 1.0)).astype(jnp.float32) * perm_scale
    )
    moments = magnetization * magnetic.astype(jnp.bfloat16)[None]
    moments_pad = padded_2(moments, (("gx", 1), ("gy", 2), ("gz", 3)), 1).astype(jnp.float32)
    source = -(central(moments_pad[0], 0) + central(moments_pad[1], 1) + central(moments_pad[2], 2))
    weights = chebyshev_weights(1.0, 0.9, SWEEPS)
    diagonal = 6.0 * permeability
    potential = weights[0] * source / diagonal
    for counter in range(1, SWEEPS):
        padded = potential_rim(potential)[1:-1, 1:-1, 1:-1]
        potential = (
            potential
            + weights[counter]
            * (source - permeability * (6.0 * potential - neighbours(padded)))
            / diagonal
        )
    force = magnet_force(moments_pad, potential_rim(potential)).astype(jnp.bfloat16)
    load = lax.all_to_all(force, "gy", split_axis=1, concat_axis=2, tiled=True).astype(jnp.float32)

    def pad_slab(field):
        rimmed = padded_2(field, ((("gx", "gy"), 1), ("gz", 3)), 1)
        return jnp.pad(rimmed, ((0, 0), (0, 0), (1, 1), (0, 0)))

    displacement = elastic_solve(load, stiffness, pad_slab)
    strain = strain_from(pad_slab(displacement)).astype(jnp.bfloat16)
    return lax.all_to_all(strain, "gy", split_axis=2, concat_axis=1, tiled=True)


def solution(mesh):
    placed = (
        P("gx", "gy", "gz"),
        P("gx", "gy", "gz"),
        P(None, "gx", "gy", "gz"),
        P(("gx", "gy"), None, "gz"),
    )
    return jax.shard_map(
        per_device, mesh=mesh, in_specs=placed, out_specs=P(None, "gx", "gy", "gz"), check_vma=False
    )
```

profile of v0, /device:TPU:0, one launch (start us, length us, event | category | flops | bytes accessed | tf_op | source)
XLA Modules:
  0.0 224.6 jit_solution(4618047857174763802)
XLA Ops:
  2.4 2.4 %collective-permute-start = (bf16[3,1,8,128]{3,2,1,0:T(8,128)(2,1)S(1)}, bf16[3,1,8,128]{3,2,1,0:T(8,128)(2,1)S(1)}, u32[]{:S(2)}, u32[]{:S(2)}) collective-permute-start(bf16[3,1,8,128]{3,2,1,0:T(8,128)(2,1)S(1)} %get-tuple-element.66), channel_id=1, source_target_pairs={{0,8},{8,16},{16,24},{1,9},{9,17},{17,25},{2,10},{10,18},{18,26},{... | collective-permute-start | bytes 18440 | tf_op jit(solution)/shard_map/ppermute | solution.py:22
  4.8 1.3 collective-permute-start.1
  6.1 3.9 %collective-permute-done.1 = bf16[3,1,8,128]{3,2,1,0:T(8,128)(2,1)S(1)} collective-permute-done((bf16[3,1,8,128]{3,2,1,0:T(8,128)(2,1)S(1)}, bf16[3,1,8,128]{3,2,1,0:T(8,128)(2,1)S(1)}, u32[]{:S(2)}, u32[]{:S(2)}) %collective-permute-start.1) | collective-permute-done | bytes 6176 | tf_op jit(solution)/shard_map/ppermute | solution.py:23
  10.5 3.4 %collective-permute-start.2 = (bf16[3,66,1,128]{1,3,2,0:T(8,128)(2,1)S(1)}, bf16[3,66,1,128]{1,3,2,0:T(8,128)(2,1)S(1)}, u32[]{:S(2)}, u32[]{:S(2)}) collective-permute-start(bf16[3,66,1,128]{1,3,2,0:T(8,128)(2,1)S(1)} %get-tuple-element.55), channel_id=1, source_target_pairs={{0,4},{1,5},{2,6},{3,7},{8,12},{9,13},{10,14},{11,15},{16,20},{17,... | collective-permute-start | bytes 152072 | tf_op jit(solution)/shard_map/ppermute | solution.py:22
  14.0 1.3 collective-permute-start.3
  16.1 4.3 %collective-permute-done.3 = bf16[3,66,1,128]{1,3,2,0:T(8,128)(2,1)S(1)} collective-permute-done((bf16[3,66,1,128]{1,3,2,0:T(8,128)(2,1)S(1)}, bf16[3,66,1,128]{1,3,2,0:T(8,128)(2,1)S(1)}, u32[]{:S(2)}, u32[]{:S(2)}) %collective-permute-start.3) | collective-permute-done | bytes 50720 | tf_op jit(solution)/shard_map/ppermute | solution.py:23
  20.5 3.5 %collective-permute-start.4 = (bf16[3,66,10,1]{1,0,3,2:T(4,128)(2,1)S(1)}, bf16[3,66,10,1]{1,0,3,2:T(4,128)(2,1)S(1)}, u32[]{:S(2)}, u32[]{:S(2)}) collective-permute-start(bf16[3,66,10,1]{1,0,3,2:T(4,128)(2,1)S(1)} %copy.93), channel_id=1, source_target_pairs={{0,1},{1,2},{2,3},{4,5},{5,6},{6,7},{8,9},{9,10},{10,11},{12,13},{... | collective-permute-start | bytes 11888 | tf_op jit(solution)/shard_map/ppermute | solution.py:22
  24.0 1.3 collective-permute-start.5
  25.6 4.0 %collective-permute-done.5 = bf16[3,66,10,1]{1,0,3,2:T(4,128)(2,1)S(1)} collective-permute-done((bf16[3,66,10,1]{1,0,3,2:T(4,128)(2,1)S(1)}, bf16[3,66,10,1]{1,0,3,2:T(4,128)(2,1)S(1)}, u32[]{:S(2)}, u32[]{:S(2)}) %collective-permute-start.5) | collective-permute-done | bytes 3992 | tf_op jit(solution)/shard_map/ppermute | solution.py:23
  31.0 1.3 collective-permute-start.6
  32.3 3.1 %collective-permute-start.7 = (f32[2,8,128]{0,2,1:T(8,128)S(1)}, f32[2,8,128]{0,2,1:T(8,128)S(1)}, u32[]{:S(2)}, u32[]{:S(2)}) collective-permute-start(f32[2,8,128]{0,2,1:T(8,128)S(1)} %get-tuple-element.64), channel_id=1, source_target_pairs={{0,8},{8,16},{16,24},{1,9},{9,17},{17,25},{2,10},{10,18},{18,26},{... | collective-permute-start | bytes 24584 | tf_op jit(solution)/shard_map/ppermute | solution.py:22
  35.4 1.5 collective-permute-done.7
  37.1 1.3 collective-permute-start.8
  38.4 4.6 %collective-permute-start.9 = (f32[68,2,128]{0,2,1:T(8,128)S(1)}, f32[68,2,128]{0,2,1:T(8,128)S(1)}, u32[]{:S(2)}, u32[]{:S(2)}) collective-permute-start(f32[68,2,128]{0,2,1:T(8,128)S(1)} %get-tuple-element.39), channel_id=1, source_target_pairs={{0,4},{1,5},{2,6},{3,7},{8,12},{9,13},{10,14},{11,15},{16,20},{17,... | collective-permute-start | bytes 208904 | tf_op jit(solution)/shard_map/ppermute | solution.py:22
  44.0 1.5 collective-permute-done.9
  45.6 1.3 collective-permute-start.10
  46.9 4.5 %collective-permute-start.11 = (f32[68,12,2]{0,2,1:T(2,128)S(1)}, f32[68,12,2]{0,2,1:T(2,128)S(1)}, u32[]{:S(2)}, u32[]{:S(2)}) collective-permute-start(f32[68,12,2]{0,2,1:T(2,128)S(1)} %get-tuple-element.34), channel_id=1, source_target_pairs={{0,1},{1,2},{2,3},{4,5},{5,6},{6,7},{8,9},{9,10},{10,11},{12,13},{... | collective-permute-start | bytes 19592 | tf_op jit(solution)/shard_map/ppermute | solution.py:22
  51.4 1.4 collective-permute-done.11
  52.8 1.7 fusion.45
  54.7 1.3 collective-permute-start.12
  56.0 6.8 %collective-permute-start.13 = (f32[2,8,128]{0,2,1:T(8,128)S(1)}, f32[2,8,128]{0,2,1:T(8,128)S(1)}, u32[]{:S(2)}, u32[]{:S(2)}) collective-permute-start(f32[2,8,128]{0,2,1:T(8,128)S(1)} %get-tuple-element.62), channel_id=1, source_target_pairs={{0,8},{8,16},{16,24},{1,9},{9,17},{17,25},{2,10},{10,18},{18,26},{... | collective-permute-start | bytes 24584 | tf_op jit(solution)/shard_map/ppermute | solution.py:22
  62.8 1.5 collective-permute-done.13
  64.5 1.3 collective-permute-start.14
  65.8 4.6 %collective-permute-start.15 = (f32[68,2,128]{0,2,1:T(8,128)S(1)}, f32[68,2,128]{0,2,1:T(8,128)S(1)}, u32[]{:S(2)}, u32[]{:S(2)}) collective-permute-start(f32[68,2,128]{0,2,1:T(8,128)S(1)} %get-tuple-element.37), channel_id=1, source_target_pairs={{0,4},{1,5},{2,6},{3,7},{8,12},{9,13},{10,14},{11,15},{16,20},{17,... | collective-permute-start | bytes 208904 | tf_op jit(solution)/shard_map/ppermute | solution.py:22
  71.4 1.5 collective-permute-done.15
  73.0 1.3 collective-permute-start.16
  74.3 4.5 %collective-permute-start.17 = (f32[68,12,2]{0,2,1:T(2,128)S(1)}, f32[68,12,2]{0,2,1:T(2,128)S(1)}, u32[]{:S(2)}, u32[]{:S(2)}) collective-permute-start(f32[68,12,2]{0,2,1:T(2,128)S(1)} %get-tuple-element.32), channel_id=1, source_target_pairs={{0,1},{1,2},{2,3},{4,5},{5,6},{6,7},{8,9},{9,10},{10,11},{12,13},{... | collective-permute-start | bytes 19592 | tf_op jit(solution)/shard_map/ppermute | solution.py:22
  78.9 1.4 collective-permute-done.17
  80.2 1.7 fusion.35
  82.1 9.6 %collective-permute-start.18 = (f32[2,8,128]{0,2,1:T(8,128)S(1)}, f32[2,8,128]{0,2,1:T(8,128)S(1)}, u32[]{:S(2)}, u32[]{:S(2)}) collective-permute-start(f32[2,8,128]{0,2,1:T(8,128)S(1)} %get-tuple-element.60), channel_id=1, source_target_pairs={{0,8},{8,16},{16,24},{1,9},{9,17},{17,25},{2,10},{10,18},{18,26},{... | collective-permute-start | bytes 24584 | tf_op jit(solution)/shard_map/ppermute | solution.py:22
  91.8 1.3 collective-permute-start.19
  93.3 6.2 %collective-permute-done.19 = f32[2,8,128]{0,2,1:T(8,128)S(1)} collective-permute-done((f32[2,8,128]{0,2,1:T(8,128)S(1)}, f32[2,8,128]{0,2,1:T(8,128)S(1)}, u32[]{:S(2)}, u32[]{:S(2)}) %collective-permute-start.19) | collective-permute-done | bytes 8224 | tf_op jit(solution)/shard_map/ppermute | solution.py:23
  99.6 4.4 %collective-permute-start.20 = (f32[68,2,128]{0,2,1:T(8,128)S(1)}, f32[68,2,128]{0,2,1:T(8,128)S(1)}, u32[]{:S(2)}, u32[]{:S(2)}) collective-permute-start(f32[68,2,128]{0,2,1:T(8,128)S(1)} %get-tuple-element.35), channel_id=1, source_target_pairs={{0,4},{1,5},{2,6},{3,7},{8,12},{9,13},{10,14},{11,15},{16,20},{17,... | collective-permute-start | bytes 208904 | tf_op jit(solution)/shard_map/ppermute | solution.py:22
  104.0 1.3 collective-permute-start.21
  105.3 1.2 collective-permute-done.20
  106.5 4.4 %collective-permute-done.21 = f32[68,2,128]{0,2,1:T(8,128)S(1)} collective-permute-done((f32[68,2,128]{0,2,1:T(8,128)S(1)}, f32[68,2,128]{0,2,1:T(8,128)S(1)}, u32[]{:S(2)}, u32[]{:S(2)}) %collective-permute-start.21) | collective-permute-done | bytes 69664 | tf_op jit(solution)/shard_map/ppermute | solution.py:23
  111.0 4.2 %collective-permute-start.22 = (f32[68,12,2]{0,2,1:T(2,128)S(1)}, f32[68,12,2]{0,2,1:T(2,128)S(1)}, u32[]{:S(2)}, u32[]{:S(2)}) collective-permute-start(f32[68,12,2]{0,2,1:T(2,128)S(1)} %get-tuple-element.29), channel_id=1, source_target_pairs={{0,1},{1,2},{2,3},{4,5},{5,6},{6,7},{8,9},{9,10},{10,11},{12,13},{... | collective-permute-start | bytes 19592 | tf_op jit(solution)/shard_map/ppermute | solution.py:22
  115.2 1.5 collective-permute-start.23
  116.7 4.1 %collective-permute-done.23 = f32[68,12,2]{0,2,1:T(2,128)S(1)} collective-permute-done((f32[68,12,2]{0,2,1:T(2,128)S(1)}, f32[68,12,2]{0,2,1:T(2,128)S(1)}, u32[]{:S(2)}, u32[]{:S(2)}) %collective-permute-start.23) | collective-permute-done | bytes 6560 | tf_op jit(solution)/shard_map/ppermute | solution.py:23
  121.1 1.6 subtract_multiply_fusion.2
  123.2 2.1 fusion.123
  126.6 3.5 %all-to-all-start = ((bf16[3,64,8,128]{3,2,0,1:T(8,128)(2,1)}), bf16[3,64,8,128]{3,2,0,1:T(8,128)(2,1)S(1)}, u32[]{:S(2)}, u32[]{:S(2)}) async-start(bf16[3,64,8,128]{3,2,0,1:T(8,128)(2,1)} %copy.99), calls=%async_computation | async-start | bytes 786432 | tf_op jit(solution)/shard_map/all_to_all | solution.py:164
  130.1 5.8 %all-to-all-done = bf16[3,64,8,128]{3,2,0,1:T(8,128)(2,1)S(1)} async-done(((bf16[3,64,8,128]{3,2,0,1:T(8,128)(2,1)}), bf16[3,64,8,128]{3,2,0,1:T(8,128)(2,1)S(1)}, u32[]{:S(2)}, u32[]{:S(2)}) %all-to-all-start) | async-done | bytes 393248 | tf_op jit(solution)/shard_map/all_to_all | solution.py:164
  136.2 1.9 collective-permute-start.24
  138.1 1.3 collective-permute-start.25
  139.6 7.3 %collective-permute-done.25 = f32[3,1,16,128]{3,2,1,0:T(8,128)S(1)} collective-permute-done((f32[3,1,16,128]{3,2,1,0:T(8,128)S(1)}, f32[3,1,16,128]{3,2,1,0:T(8,128)S(1)}, u32[]{:S(2)}, u32[]{:S(2)}) %collective-permute-start.25) | collective-permute-done | bytes 24608 | tf_op jit(solution)/shard_map/ppermute | solution.py:23
  147.7 3.6 %collective-permute-start.26 = (f32[3,34,16,1]{1,2,3,0:T(8,128)S(1)}, f32[3,34,16,1]{1,2,3,0:T(8,128)S(1)}, u32[]{:S(2)}, u32[]{:S(2)}) collective-permute-start(f32[3,34,16,1]{1,2,3,0:T(8,128)S(1)} %copy.102), channel_id=1, source_target_pairs={{0,1},{1,2},{2,3},{4,5},{5,6},{6,7},{8,9},{9,10},{10,11},{12,13},{... | collective-permute-start | bytes 19592 | tf_op jit(solution)/shard_map/ppermute | solution.py:22
  151.8 1.3 collective-permute-start.27
  153.6 3.9 %collective-permute-done.27 = f32[3,34,16,1]{1,2,3,0:T(8,128)S(1)} collective-permute-done((f32[3,34,16,1]{1,2,3,0:T(8,128)S(1)}, f32[3,34,16,1]{1,2,3,0:T(8,128)S(1)}, u32[]{:S(2)}, u32[]{:S(2)}) %collective-permute-start.27) | collective-permute-done | bytes 6560 | tf_op jit(solution)/shard_map/ppermute | solution.py:23
  162.5 3.3 %collective-permute-start.28 = (f32[3,1,16,128]{3,2,1,0:T(8,128)S(1)}, f32[3,1,16,128]{3,2,1,0:T(8,128)S(1)}, u32[]{:S(2)}, u32[]{:S(2)}) collective-permute-start(f32[3,1,16,128]{3,2,1,0:T(8,128)S(1)} %get-tuple-element.51), channel_id=1, source_target_pairs={{0,4},{4,8},{8,12},{12,16},{16,20},{20,24},{24,28},{1,5},{5,9},{9,... | collective-permute-start | bytes 73736 | tf_op jit(solution)/shard_map/ppermute | solution.py:22
  165.8 1.5 collective-permute-start.29
  167.3 4.2 %collective-permute-done.29 = f32[3,1,16,128]{3,2,1,0:T(8,128)S(1)} collective-permute-done((f32[3,1,16,128]{3,2,1,0:T(8,128)S(1)}, f32[3,1,16,128]{3,2,1,0:T(8,128)S(1)}, u32[]{:S(2)}, u32[]{:S(2)}) %collective-permute-start.29) | collective-permute-done | bytes 24608 | tf_op jit(solution)/shard_map/ppermute | solution.py:23
  172.3 3.5 %collective-permute-start.30 = (f32[3,34,16,1]{1,2,3,0:T(8,128)S(1)}, f32[3,34,16,1]{1,2,3,0:T(8,128)S(1)}, u32[]{:S(2)}, u32[]{:S(2)}) collective-permute-start(f32[3,34,16,1]{1,2,3,0:T(8,128)S(1)} %copy.106), channel_id=1, source_target_pairs={{0,1},{1,2},{2,3},{4,5},{5,6},{6,7},{8,9},{9,10},{10,11},{12,13},{... | collective-permute-start | bytes 19592 | tf_op jit(solution)/shard_map/ppermute | solution.py:22
  176.3 1.3 collective-permute-start.31
  178.1 3.9 %collective-permute-done.31 = f32[3,34,16,1]{1,2,3,0:T(8,128)S(1)} collective-permute-done((f32[3,34,16,1]{1,2,3,0:T(8,128)S(1)}, f32[3,34,16,1]{1,2,3,0:T(8,128)S(1)}, u32[]{:S(2)}, u32[]{:S(2)}) %collective-permute-start.31) | collective-permute-done | bytes 6560 | tf_op jit(solution)/shard_map/ppermute | solution.py:23
  187.1 4.1 %collective-permute-start.32 = (f32[3,1,16,128]{3,2,1,0:T(8,128)S(1)}, f32[3,1,16,128]{3,2,1,0:T(8,128)S(1)}, u32[]{:S(2)}, u32[]{:S(2)}) collective-permute-start(f32[3,1,16,128]{3,2,1,0:T(8,128)S(1)} %get-tuple-element.49), channel_id=1, source_target_pairs={{0,4},{4,8},{8,12},{12,16},{16,20},{20,24},{24,28},{1,5},{5,9},{9,... | collective-permute-start | bytes 73736 | tf_op jit(solution)/shard_map/ppermute | solution.py:22
  191.2 1.3 collective-permute-start.33
  192.7 4.4 %collective-permute-done.33 = f32[3,1,16,128]{3,2,1,0:T(8,128)S(1)} collective-permute-done((f32[3,1,16,128]{3,2,1,0:T(8,128)S(1)}, f32[3,1,16,128]{3,2,1,0:T(8,128)S(1)}, u32[]{:S(2)}, u32[]{:S(2)}) %collective-permute-start.33) | collective-permute-done | bytes 24608 | tf_op jit(solution)/shard_map/ppermute | solution.py:23
  197.9 2.2 collective-permute-start.34
  200.5 1.3 collective-permute-start.35
  202.3 3.9 %collective-permute-done.35 = f32[3,34,16,1]{1,2,3,0:T(8,128)S(1)} collective-permute-done((f32[3,34,16,1]{1,2,3,0:T(8,128)S(1)}, f32[3,34,16,1]{1,2,3,0:T(8,128)S(1)}, u32[]{:S(2)}, u32[]{:S(2)}) %collective-permute-start.35) | collective-permute-done | bytes 6560 | tf_op jit(solution)/shard_map/ppermute | solution.py:23
  206.8 1.2 select_maximum_fusion
  210.0 13.2 %all_to_all.27 = bf16[6,32,16,128]{3,1,0,2:T(8,128)(2,1)S(1)} all-to-all(bf16[6,32,16,128]{3,1,0,2:T(8,128)(2,1)S(1)} %copy.114), channel_id=1, replica_groups=mesh['gx'=4,'gy'=2,'gz'=4] {'gy'}, dimensions={2} | all-to-all | bytes 1572864 | tf_op jit(solution)/shard_map/all_to_all | solution.py:172
  223.2 1.4 copy.116
  (107 shorter events, 29.5 us)
Async XLA Ops:
  1.2 24.1 %copy-start.7 = (f32[64,8,128]{2,1,0:T(8,128)S(1)}, f32[64,8,128]{2,1,0:T(8,128)}, u32[]{:S(2)}) copy-start(f32[64,8,128]{2,1,0:T(8,128)} %param.5) | copy-start | bytes 786436
  2.4 3.7 %collective-permute-start = (bf16[3,1,8,128]{3,2,1,0:T(8,128)(2,1)S(1)}, bf16[3,1,8,128]{3,2,1,0:T(8,128)(2,1)S(1)}, u32[]{:S(2)}, u32[]{:S(2)}) collective-permute-start(bf16[3,1,8,128]{3,2,1,0:T(8,128)(2,1)S(1)} %get-tuple-element.66), channel_id=1, source_target_pairs={{0,8},{8,16},{16,24},{1,9},{9,17},{17,25},{2,10},{10,18},{18,26},{... | collective-permute-start | bytes 18440 | tf_op jit(solution)/shard_map/ppermute | solution.py:22
  4.8 5.2 %collective-permute-start.1 = (bf16[3,1,8,128]{3,2,1,0:T(8,128)(2,1)S(1)}, bf16[3,1,8,128]{3,2,1,0:T(8,128)(2,1)S(1)}, u32[]{:S(2)}, u32[]{:S(2)}) collective-permute-start(bf16[3,1,8,128]{3,2,1,0:T(8,128)(2,1)S(1)} %get-tuple-element.67), channel_id=1, source_target_pairs={{8,0},{16,8},{24,16},{9,1},{17,9},{25,17},{10,2},{18,10},{26,18},{... | collective-permute-start | bytes 18440 | tf_op jit(solution)/shard_map/ppermute | solution.py:23
  10.5 5.6 %collective-permute-start.2 = (bf16[3,66,1,128]{1,3,2,0:T(8,128)(2,1)S(1)}, bf16[3,66,1,128]{1,3,2,0:T(8,128)(2,1)S(1)}, u32[]{:S(2)}, u32[]{:S(2)}) collective-permute-start(bf16[3,66,1,128]{1,3,2,0:T(8,128)(2,1)S(1)} %get-tuple-element.55), channel_id=1, source_target_pairs={{0,4},{1,5},{2,6},{3,7},{8,12},{9,13},{10,14},{11,15},{16,20},{17,... | collective-permute-start | bytes 152072 | tf_op jit(solution)/shard_map/ppermute | solution.py:22
  14.0 6.5 %collective-permute-start.3 = (bf16[3,66,1,128]{1,3,2,0:T(8,128)(2,1)S(1)}, bf16[3,66,1,128]{1,3,2,0:T(8,128)(2,1)S(1)}, u32[]{:S(2)}, u32[]{:S(2)}) collective-permute-start(bf16[3,66,1,128]{1,3,2,0:T(8,128)(2,1)S(1)} %get-tuple-element.56), channel_id=1, source_target_pairs={{4,0},{5,1},{6,2},{7,3},{12,8},{13,9},{14,10},{15,11},{20,16},{21,... | collective-permute-start | bytes 152072 | tf_op jit(solution)/shard_map/ppermute | solution.py:23
  20.5 5.0 %collective-permute-start.4 = (bf16[3,66,10,1]{1,0,3,2:T(4,128)(2,1)S(1)}, bf16[3,66,10,1]{1,0,3,2:T(4,128)(2,1)S(1)}, u32[]{:S(2)}, u32[]{:S(2)}) collective-permute-start(bf16[3,66,10,1]{1,0,3,2:T(4,128)(2,1)S(1)} %copy.93), channel_id=1, source_target_pairs={{0,1},{1,2},{2,3},{4,5},{5,6},{6,7},{8,9},{9,10},{10,11},{12,13},{... | collective-permute-start | bytes 11888 | tf_op jit(solution)/shard_map/ppermute | solution.py:22
  24.0 5.6 %collective-permute-start.5 = (bf16[3,66,10,1]{1,0,3,2:T(4,128)(2,1)S(1)}, bf16[3,66,10,1]{1,0,3,2:T(4,128)(2,1)S(1)}, u32[]{:S(2)}, u32[]{:S(2)}) collective-permute-start(bf16[3,66,10,1]{1,0,3,2:T(4,128)(2,1)S(1)} %copy.94), channel_id=1, source_target_pairs={{1,0},{2,1},{3,2},{5,4},{6,5},{7,6},{9,8},{10,9},{11,10},{13,12},{... | collective-permute-start | bytes 11888 | tf_op jit(solution)/shard_map/ppermute | solution.py:23
  31.0 4.4 %collective-permute-start.6 = (f32[2,8,128]{0,2,1:T(8,128)S(1)}, f32[2,8,128]{0,2,1:T(8,128)S(1)}, u32[]{:S(2)}, u32[]{:S(2)}) collective-permute-start(f32[2,8,128]{0,2,1:T(8,128)S(1)} %get-tuple-element.65), channel_id=1, source_target_pairs={{8,0},{16,8},{24,16},{9,1},{17,9},{25,17},{10,2},{18,10},{26,18},{... | collective-permute-start | bytes 24584 | tf_op jit(solution)/shard_map/ppermute | solution.py:23
  32.3 4.6 %collective-permute-start.7 = (f32[2,8,128]{0,2,1:T(8,128)S(1)}, f32[2,8,128]{0,2,1:T(8,128)S(1)}, u32[]{:S(2)}, u32[]{:S(2)}) collective-permute-start(f32[2,8,128]{0,2,1:T(8,128)S(1)} %get-tuple-element.64), channel_id=1, source_target_pairs={{0,8},{8,16},{16,24},{1,9},{9,17},{17,25},{2,10},{10,18},{18,26},{... | collective-permute-start | bytes 24584 | tf_op jit(solution)/shard_map/ppermute | solution.py:22
  37.1 6.9 %collective-permute-start.8 = (f32[68,2,128]{0,2,1:T(8,128)S(1)}, f32[68,2,128]{0,2,1:T(8,128)S(1)}, u32[]{:S(2)}, u32[]{:S(2)}) collective-permute-start(f32[68,2,128]{0,2,1:T(8,128)S(1)} %get-tuple-element.40), channel_id=1, source_target_pairs={{4,0},{5,1},{6,2},{7,3},{12,8},{13,9},{14,10},{15,11},{20,16},{21,... | collective-permute-start | bytes 208904 | tf_op jit(solution)/shard_map/ppermute | solution.py:23
  38.4 7.1 %collective-permute-start.9 = (f32[68,2,128]{0,2,1:T(8,128)S(1)}, f32[68,2,128]{0,2,1:T(8,128)S(1)}, u32[]{:S(2)}, u32[]{:S(2)}) collective-permute-start(f32[68,2,128]{0,2,1:T(8,128)S(1)} %get-tuple-element.39), channel_id=1, source_target_pairs={{0,4},{1,5},{2,6},{3,7},{8,12},{9,13},{10,14},{11,15},{16,20},{17,... | collective-permute-start | bytes 208904 | tf_op jit(solution)/shard_map/ppermute | solution.py:22
  45.6 5.9 %collective-permute-start.10 = (f32[68,12,2]{0,2,1:T(2,128)S(1)}, f32[68,12,2]{0,2,1:T(2,128)S(1)}, u32[]{:S(2)}, u32[]{:S(2)}) collective-permute-start(f32[68,12,2]{0,2,1:T(2,128)S(1)} %get-tuple-element.33), channel_id=1, source_target_pairs={{1,0},{2,1},{3,2},{5,4},{6,5},{7,6},{9,8},{10,9},{11,10},{13,12},{... | collective-permute-start | bytes 19592 | tf_op jit(solution)/shard_map/ppermute | solution.py:23
  46.9 5.9 %collective-permute-start.11 = (f32[68,12,2]{0,2,1:T(2,128)S(1)}, f32[68,12,2]{0,2,1:T(2,128)S(1)}, u32[]{:S(2)}, u32[]{:S(2)}) collective-permute-start(f32[68,12,2]{0,2,1:T(2,128)S(1)} %get-tuple-element.34), channel_id=1, source_target_pairs={{0,1},{1,2},{2,3},{4,5},{5,6},{6,7},{8,9},{9,10},{10,11},{12,13},{... | collective-permute-start | bytes 19592 | tf_op jit(solution)/shard_map/ppermute | solution.py:22
  54.7 8.1 %collective-permute-start.12 = (f32[2,8,128]{0,2,1:T(8,128)S(1)}, f32[2,8,128]{0,2,1:T(8,128)S(1)}, u32[]{:S(2)}, u32[]{:S(2)}) collective-permute-start(f32[2,8,128]{0,2,1:T(8,128)S(1)} %get-tuple-element.63), channel_id=1, source_target_pairs={{8,0},{16,8},{24,16},{9,1},{17,9},{25,17},{10,2},{18,10},{26,18},{... | collective-permute-start | bytes 24584 | tf_op jit(solution)/shard_map/ppermute | solution.py:23
  56.0 8.3 %collective-permute-start.13 = (f32[2,8,128]{0,2,1:T(8,128)S(1)}, f32[2,8,128]{0,2,1:T(8,128)S(1)}, u32[]{:S(2)}, u32[]{:S(2)}) collective-permute-start(f32[2,8,128]{0,2,1:T(8,128)S(1)} %get-tuple-element.62), channel_id=1, source_target_pairs={{0,8},{8,16},{16,24},{1,9},{9,17},{17,25},{2,10},{10,18},{18,26},{... | collective-permute-start | bytes 24584 | tf_op jit(solution)/shard_map/ppermute | solution.py:22
  64.5 6.9 %collective-permute-start.14 = (f32[68,2,128]{0,2,1:T(8,128)S(1)}, f32[68,2,128]{0,2,1:T(8,128)S(1)}, u32[]{:S(2)}, u32[]{:S(2)}) collective-permute-start(f32[68,2,128]{0,2,1:T(8,128)S(1)} %get-tuple-element.38), channel_id=1, source_target_pairs={{4,0},{5,1},{6,2},{7,3},{12,8},{13,9},{14,10},{15,11},{20,16},{21,... | collective-permute-start | bytes 208904 | tf_op jit(solution)/shard_map/ppermute | solution.py:23
  65.8 7.1 %collective-permute-start.15 = (f32[68,2,128]{0,2,1:T(8,128)S(1)}, f32[68,2,128]{0,2,1:T(8,128)S(1)}, u32[]{:S(2)}, u32[]{:S(2)}) collective-permute-start(f32[68,2,128]{0,2,1:T(8,128)S(1)} %get-tuple-element.37), channel_id=1, source_target_pairs={{0,4},{1,5},{2,6},{3,7},{8,12},{9,13},{10,14},{11,15},{16,20},{17,... | collective-permute-start | bytes 208904 | tf_op jit(solution)/shard_map/ppermute | solution.py:22
  73.0 5.9 %collective-permute-start.16 = (f32[68,12,2]{0,2,1:T(2,128)S(1)}, f32[68,12,2]{0,2,1:T(2,128)S(1)}, u32[]{:S(2)}, u32[]{:S(2)}) collective-permute-start(f32[68,12,2]{0,2,1:T(2,128)S(1)} %get-tuple-element.31), channel_id=1, source_target_pairs={{1,0},{2,1},{3,2},{5,4},{6,5},{7,6},{9,8},{10,9},{11,10},{13,12},{... | collective-permute-start | bytes 19592 | tf_op jit(solution)/shard_map/ppermute | solution.py:23
  74.3 5.9 %collective-permute-start.17 = (f32[68,12,2]{0,2,1:T(2,128)S(1)}, f32[68,12,2]{0,2,1:T(2,128)S(1)}, u32[]{:S(2)}, u32[]{:S(2)}) collective-permute-start(f32[68,12,2]{0,2,1:T(2,128)S(1)} %get-tuple-element.32), channel_id=1, source_target_pairs={{0,1},{1,2},{2,3},{4,5},{5,6},{6,7},{8,9},{9,10},{10,11},{12,13},{... | collective-permute-start | bytes 19592 | tf_op jit(solution)/shard_map/ppermute | solution.py:22
  82.1 11.1 %collective-permute-start.18 = (f32[2,8,128]{0,2,1:T(8,128)S(1)}, f32[2,8,128]{0,2,1:T(8,128)S(1)}, u32[]{:S(2)}, u32[]{:S(2)}) collective-permute-start(f32[2,8,128]{0,2,1:T(8,128)S(1)} %get-tuple-element.60), channel_id=1, source_target_pairs={{0,8},{8,16},{16,24},{1,9},{9,17},{17,25},{2,10},{10,18},{18,26},{... | collective-permute-start | bytes 24584 | tf_op jit(solution)/shard_map/ppermute | solution.py:22
  91.8 7.7 %collective-permute-start.19 = (f32[2,8,128]{0,2,1:T(8,128)S(1)}, f32[2,8,128]{0,2,1:T(8,128)S(1)}, u32[]{:S(2)}, u32[]{:S(2)}) collective-permute-start(f32[2,8,128]{0,2,1:T(8,128)S(1)} %get-tuple-element.61), channel_id=1, source_target_pairs={{8,0},{16,8},{24,16},{9,1},{17,9},{25,17},{10,2},{18,10},{26,18},{... | collective-permute-start | bytes 24584 | tf_op jit(solution)/shard_map/ppermute | solution.py:23
  99.6 6.9 %collective-permute-start.20 = (f32[68,2,128]{0,2,1:T(8,128)S(1)}, f32[68,2,128]{0,2,1:T(8,128)S(1)}, u32[]{:S(2)}, u32[]{:S(2)}) collective-permute-start(f32[68,2,128]{0,2,1:T(8,128)S(1)} %get-tuple-element.35), channel_id=1, source_target_pairs={{0,4},{1,5},{2,6},{3,7},{8,12},{9,13},{10,14},{11,15},{16,20},{17,... | collective-permute-start | bytes 208904 | tf_op jit(solution)/shard_map/ppermute | solution.py:22
  104.0 6.9 %collective-permute-start.21 = (f32[68,2,128]{0,2,1:T(8,128)S(1)}, f32[68,2,128]{0,2,1:T(8,128)S(1)}, u32[]{:S(2)}, u32[]{:S(2)}) collective-permute-start(f32[68,2,128]{0,2,1:T(8,128)S(1)} %get-tuple-element.36), channel_id=1, source_target_pairs={{4,0},{5,1},{6,2},{7,3},{12,8},{13,9},{14,10},{15,11},{20,16},{21,... | collective-permute-start | bytes 208904 | tf_op jit(solution)/shard_map/ppermute | solution.py:23
  111.0 5.7 %collective-permute-start.22 = (f32[68,12,2]{0,2,1:T(2,128)S(1)}, f32[68,12,2]{0,2,1:T(2,128)S(1)}, u32[]{:S(2)}, u32[]{:S(2)}) collective-permute-start(f32[68,12,2]{0,2,1:T(2,128)S(1)} %get-tuple-element.29), channel_id=1, source_target_pairs={{0,1},{1,2},{2,3},{4,5},{5,6},{6,7},{8,9},{9,10},{10,11},{12,13},{... | collective-permute-start | bytes 19592 | tf_op jit(solution)/shard_map/ppermute | solution.py:22
  115.2 5.6 %collective-permute-start.23 = (f32[68,12,2]{0,2,1:T(2,128)S(1)}, f32[68,12,2]{0,2,1:T(2,128)S(1)}, u32[]{:S(2)}, u32[]{:S(2)}) collective-permute-start(f32[68,12,2]{0,2,1:T(2,128)S(1)} %get-tuple-element.30), channel_id=1, source_target_pairs={{1,0},{2,1},{3,2},{5,4},{6,5},{7,6},{9,8},{10,9},{11,10},{13,12},{... | collective-permute-start | bytes 19592 | tf_op jit(solution)/shard_map/ppermute | solution.py:23
  125.4 4.7 %copy-start.4 = (f32[32,16,128]{2,1,0:T(8,128)S(1)}, f32[32,16,128]{2,1,0:T(8,128)}, u32[]{:S(2)}) copy-start(f32[32,16,128]{2,1,0:T(8,128)} %param.7) | copy-start | bytes 786436
  126.6 9.3 %all-to-all-start = ((bf16[3,64,8,128]{3,2,0,1:T(8,128)(2,1)}), bf16[3,64,8,128]{3,2,0,1:T(8,128)(2,1)S(1)}, u32[]{:S(2)}, u32[]{:S(2)}) async-start(bf16[3,64,8,128]{3,2,0,1:T(8,128)(2,1)} %copy.99), calls=%async_computation | async-start | bytes 786432 | tf_op jit(solution)/shard_map/all_to_all | solution.py:164
  136.2 3.4 %collective-permute-start.24 = (f32[3,1,16,128]{3,2,1,0:T(8,128)S(1)}, f32[3,1,16,128]{3,2,1,0:T(8,128)S(1)}, u32[]{:S(2)}, u32[]{:S(2)}) collective-permute-start(f32[3,1,16,128]{3,2,1,0:T(8,128)S(1)} %get-tuple-element.53), channel_id=1, source_target_pairs={{0,4},{4,8},{8,12},{12,16},{16,20},{20,24},{24,28},{1,5},{5,9},{9,... | collective-permute-start | bytes 73736 | tf_op jit(solution)/shard_map/ppermute | solution.py:22
  138.1 8.8 %collective-permute-start.25 = (f32[3,1,16,128]{3,2,1,0:T(8,128)S(1)}, f32[3,1,16,128]{3,2,1,0:T(8,128)S(1)}, u32[]{:S(2)}, u32[]{:S(2)}) collective-permute-start(f32[3,1,16,128]{3,2,1,0:T(8,128)S(1)} %get-tuple-element.54), channel_id=1, source_target_pairs={{4,0},{8,4},{12,8},{16,12},{20,16},{24,20},{28,24},{5,1},{9,5},{13... | collective-permute-start | bytes 73736 | tf_op jit(solution)/shard_map/ppermute | solution.py:23
  147.7 5.4 %collective-permute-start.26 = (f32[3,34,16,1]{1,2,3,0:T(8,128)S(1)}, f32[3,34,16,1]{1,2,3,0:T(8,128)S(1)}, u32[]{:S(2)}, u32[]{:S(2)}) collective-permute-start(f32[3,34,16,1]{1,2,3,0:T(8,128)S(1)} %copy.102), channel_id=1, source_target_pairs={{0,1},{1,2},{2,3},{4,5},{5,6},{6,7},{8,9},{9,10},{10,11},{12,13},{... | collective-permute-start | bytes 19592 | tf_op jit(solution)/shard_map/ppermute | solution.py:22
  151.8 5.7 %collective-permute-start.27 = (f32[3,34,16,1]{1,2,3,0:T(8,128)S(1)}, f32[3,34,16,1]{1,2,3,0:T(8,128)S(1)}, u32[]{:S(2)}, u32[]{:S(2)}) collective-permute-start(f32[3,34,16,1]{1,2,3,0:T(8,128)S(1)} %copy.103), channel_id=1, source_target_pairs={{1,0},{2,1},{3,2},{5,4},{6,5},{7,6},{9,8},{10,9},{11,10},{13,12},{... | collective-permute-start | bytes 19592 | tf_op jit(solution)/shard_map/ppermute | solution.py:23
  161.2 1.3 copy-start
  161.2 1.0 copy-start.5
  162.2 9.3 %copy-start.2 = (f32[1,32,16,128]{3,2,1,0:T(8,128)}, f32[1,32,16,128]{3,2,1,0:T(8,128)S(1)}, u32[]{:S(2)}) copy-start(f32[1,32,16,128]{3,2,1,0:T(8,128)S(1)} %fusion.100) | copy-start | bytes 786436
  162.5 4.9 %collective-permute-start.28 = (f32[3,1,16,128]{3,2,1,0:T(8,128)S(1)}, f32[3,1,16,128]{3,2,1,0:T(8,128)S(1)}, u32[]{:S(2)}, u32[]{:S(2)}) collective-permute-start(f32[3,1,16,128]{3,2,1,0:T(8,128)S(1)} %get-tuple-element.51), channel_id=1, source_target_pairs={{0,4},{4,8},{8,12},{12,16},{16,20},{20,24},{24,28},{1,5},{5,9},{9,... | collective-permute-start | bytes 73736 | tf_op jit(solution)/shard_map/ppermute | solution.py:22
  165.8 5.7 %collective-permute-start.29 = (f32[3,1,16,128]{3,2,1,0:T(8,128)S(1)}, f32[3,1,16,128]{3,2,1,0:T(8,128)S(1)}, u32[]{:S(2)}, u32[]{:S(2)}) collective-permute-start(f32[3,1,16,128]{3,2,1,0:T(8,128)S(1)} %get-tuple-element.52), channel_id=1, source_target_pairs={{4,0},{8,4},{12,8},{16,12},{20,16},{24,20},{28,24},{5,1},{9,5},{13... | collective-permute-start | bytes 73736 | tf_op jit(solution)/shard_map/ppermute | solution.py:23
  172.3 5.2 %collective-permute-start.30 = (f32[3,34,16,1]{1,2,3,0:T(8,128)S(1)}, f32[3,34,16,1]{1,2,3,0:T(8,128)S(1)}, u32[]{:S(2)}, u32[]{:S(2)}) collective-permute-start(f32[3,34,16,1]{1,2,3,0:T(8,128)S(1)} %copy.106), channel_id=1, source_target_pairs={{0,1},{1,2},{2,3},{4,5},{5,6},{6,7},{8,9},{9,10},{10,11},{12,13},{... | collective-permute-start | bytes 19592 | tf_op jit(solution)/shard_map/ppermute | solution.py:22
  176.3 5.7 %collective-permute-start.31 = (f32[3,34,16,1]{1,2,3,0:T(8,128)S(1)}, f32[3,34,16,1]{1,2,3,0:T(8,128)S(1)}, u32[]{:S(2)}, u32[]{:S(2)}) collective-permute-start(f32[3,34,16,1]{1,2,3,0:T(8,128)S(1)} %copy.107), channel_id=1, source_target_pairs={{1,0},{2,1},{3,2},{5,4},{6,5},{7,6},{9,8},{10,9},{11,10},{13,12},{... | collective-permute-start | bytes 19592 | tf_op jit(solution)/shard_map/ppermute | solution.py:23
  185.6 1.0 copy-start.1
  185.6 1.0 copy-start.3
  185.6 1.1 copy-start.6
  187.1 5.6 %collective-permute-start.32 = (f32[3,1,16,128]{3,2,1,0:T(8,128)S(1)}, f32[3,1,16,128]{3,2,1,0:T(8,128)S(1)}, u32[]{:S(2)}, u32[]{:S(2)}) collective-permute-start(f32[3,1,16,128]{3,2,1,0:T(8,128)S(1)} %get-tuple-element.49), channel_id=1, source_target_pairs={{0,4},{4,8},{8,12},{12,16},{16,20},{20,24},{24,28},{1,5},{5,9},{9,... | collective-permute-start | bytes 73736 | tf_op jit(solution)/shard_map/ppermute | solution.py:22
  191.2 5.9 %collective-permute-start.33 = (f32[3,1,16,128]{3,2,1,0:T(8,128)S(1)}, f32[3,1,16,128]{3,2,1,0:T(8,128)S(1)}, u32[]{:S(2)}, u32[]{:S(2)}) collective-permute-start(f32[3,1,16,128]{3,2,1,0:T(8,128)S(1)} %get-tuple-element.50), channel_id=1, source_target_pairs={{4,0},{8,4},{12,8},{16,12},{20,16},{24,20},{28,24},{5,1},{9,5},{13... | collective-permute-start | bytes 73736 | tf_op jit(solution)/shard_map/ppermute | solution.py:23
  197.9 3.9 %collective-permute-start.34 = (f32[3,34,16,1]{1,2,3,0:T(8,128)S(1)}, f32[3,34,16,1]{1,2,3,0:T(8,128)S(1)}, u32[]{:S(2)}, u32[]{:S(2)}) collective-permute-start(f32[3,34,16,1]{1,2,3,0:T(8,128)S(1)} %copy.110), channel_id=1, source_target_pairs={{0,1},{1,2},{2,3},{4,5},{5,6},{6,7},{8,9},{9,10},{10,11},{12,13},{... | collective-permute-start | bytes 19592 | tf_op jit(solution)/shard_map/ppermute | solution.py:22
  200.5 5.7 %collective-permute-start.35 = (f32[3,34,16,1]{1,2,3,0:T(8,128)S(1)}, f32[3,34,16,1]{1,2,3,0:T(8,128)S(1)}, u32[]{:S(2)}, u32[]{:S(2)}) collective-permute-start(f32[3,34,16,1]{1,2,3,0:T(8,128)S(1)} %copy.111), channel_id=1, source_target_pairs={{1,0},{2,1},{3,2},{5,4},{6,5},{7,6},{9,8},{10,9},{11,10},{13,12},{... | collective-permute-start | bytes 19592 | tf_op jit(solution)/shard_map/ppermute | solution.py:23
where the time goes:
time: 226 us; the launch traced here: 225 us
  starting transfers between devices  101 us (45%)
  waiting for transfers between devices  73.7 us (33%)
  other arithmetic  22.4 us (10%)
  local copies, waits for them, and re-layouts  13.2 us (6%)
  blocking collectives  13.2 us (6%)
    ppermute x18, starting transfers between devices, padded_2(): before = lax.ppermute(last, axis, up)  74.2 us
    ppermute x18, waiting for transfers between devices, padded_2(): after = lax.ppermute(leading, axis, down)  56.5 us
    ppermute x18, starting transfers between devices, padded_2(): after = lax.ppermute(leading, axis, down)  23.6 us
    all_to_all x1, blocking collectives, per_device(): return lax.all_to_all(strain, 'gy', split_axis=2, concat_axis=1, tiled=True)  13.2 us
    ppermute x18, waiting for transfers between devices, padded_2(): before = lax.ppermute(last, axis, up)  11.4 us
    all_to_all x1, waiting for transfers between devices, per_device(): lax.all_to_all(force, 'gy', split_axis=1, concat_axis=2, tiled=True)  5.82 us
    another operation x6, other arithmetic, navier(): return jnp.stack(result)  5.01 us
    concatenate x10, other arithmetic, padded_2(): value = jnp.concatenate([before, value, after], axis=dim)  4.53 us
  transfers between devices with their start and end apart: 37, of which 26 were waited for; matrix products, arithmetic and copies ran while one was open for 1% of the time, Pallas kernels for 0%

commit v1 on v0

v1 whole, which is shorter than its diff:
```python
import functools
import math

import jax
import jax.numpy as jnp
from jax import lax
from jax.experimental import pallas as pl
from jax.experimental.pallas import tpu as pltpu
from jax.sharding import PartitionSpec as P

SWEEPS = 3
STRAIN_PAIRS = ((0, 0), (1, 1), (2, 2), (0, 1), (1, 2), (0, 2))
STRESS_AT = {(0, 0): 0, (1, 1): 1, (2, 2): 2, (0, 1): 3, (1, 0): 3, (1, 2): 4, (2, 1): 4, (0, 2): 5, (2, 0): 5}
MAGNETO = 4.0
MESH = pl.DeviceIdType.MESH
RIM = 4


def chebyshev_weights(middle, radius, count):
    return [
        1.0 / (middle + radius * math.cos((2 * counter + 1) * math.pi / (2 * count)))
        for counter in range(count)
    ]


def shift(value, dimension, step):
    size = value.shape[dimension]
    return pltpu.roll(value, (-step) % size, dimension)


def sides(value, dimension):
    return shift(value, dimension, 1), shift(value, dimension, -1)


def kernel(sizes, phase, perm, magnet, stiff, out, flat, diag, mom, src, pot1, pot2, stress, load, disp1, disp2,
           mask, modulus, rx_m, rx_s, rx_g, tz_m, tz_s, tz_g, rz_m, rz_s, rz_g, send_sem, recv_sem, g_send, g_recv, g_local):
    nx, ny, nz, X, Y, Z = sizes
    XR, ZR = X + 2 * RIM, 2 * Z
    gx, gy, gz = lax.axis_index("gx"), lax.axis_index("gy"), lax.axis_index("gz")
    place = {"gx": gx, "gy": gy, "gz": gz}
    count = {"gx": nx, "gy": ny, "gz": nz}

    def has(axis, side):
        return place[axis] > 0 if side == 0 else place[axis] < count[axis] - 1

    def device(axis, index):
        at = dict(place)
        at[axis] = index
        return (at["gx"], at["gy"], at["gz"])

    def beside(axis, side):
        return device(axis, place[axis] + (-1 if side == 0 else 1))

    barrier = pltpu.get_barrier_semaphore()
    greeted = 0
    for axis in ("gx", "gz"):
        for side in (0, 1):
            @pl.when(has(axis, side))
            def _():
                pl.semaphore_signal(barrier, inc=1, device_id=beside(axis, side), device_id_type=MESH)
            greeted = greeted + has(axis, side).astype(jnp.int32)
    for k in range(1, ny):
        pl.semaphore_signal(barrier, inc=1, device_id=device("gy", lax.rem(gy + k, ny)), device_id_type=MESH)
    greeted = greeted + (ny - 1)

    for c in range(3):
        flat[c] = magnet[c].astype(jnp.float32)
    for y in range(Y):
        rows = pl.ds(y, X, stride=Y)
        kind = phase[rows, :]
        magnetic = kind == 0
        mu = jnp.where(magnetic, 4.0, jnp.where(kind == 1, 1.5, 1.0)).astype(jnp.float32) * perm[rows, :]
        diag[y] = 6.0 * mu
        for c in range(3):
            mom[c, RIM + y, 0:X, 0:Z] = jnp.where(magnetic, flat[c, rows, :], 0.0)

    row = lax.broadcasted_iota(jnp.int32, (XR, ZR), 0)
    lane = lax.broadcasted_iota(jnp.int32, (XR, ZR), 1)
    real = ((row < X) | ((row < X + RIM) & has("gx", 1)) | ((row >= X + RIM) & has("gx", 0))) & (
        (lane < Z) | ((lane < Z + Z // 2) & has("gz", 1)) | ((lane >= Z + Z // 2) & has("gz", 0)))
    mask[...] = jnp.where(real, 1.0, 0.0)

    for buffer in (rx_m, rx_s, rx_g):
        for side in (0, 1):
            @pl.when(jnp.logical_not(has("gx", side)))
            def _():
                buffer[side] = jnp.zeros(buffer.shape[1:], jnp.float32)
    for buffer in (rz_m, rz_s, rz_g):
        for side in (0, 1):
            @pl.when(jnp.logical_not(has("gz", side)))
            def _():
                buffer[side] = jnp.zeros(buffer.shape[1:], jnp.float32)
    for buffer in (mom, src, load):
        for side, first in ((0, 0), (1, RIM + Y)):
            @pl.when(jnp.logical_not(has("gy", side)))
            def _():
                for c in range(3 if buffer is not src else 1):
                    buffer[c, first:first + RIM] = jnp.zeros((RIM, XR, ZR), jnp.float32)

    pl.semaphore_wait(barrier, greeted)

    span = X // ny
    for k in range(1, ny):
        peer = lax.rem(gy + k, ny)
        pltpu.make_async_remote_copy(
            src_ref=stiff.at[:, pl.ds(pl.multiple_of(peer * Y, Y), Y), :],
            dst_ref=modulus.at[pl.ds(gy * span, span)],
            send_sem=g_send.at[k], recv_sem=g_recv.at[k],
            device_id=device("gy", peer), device_id_type=MESH).start()
    own = pltpu.make_async_copy(
        stiff.at[:, pl.ds(pl.multiple_of(gy * Y, Y), Y), :], modulus.at[pl.ds(gy * span, span)], g_local)
    own.start()

    def swap(axis, which, pairs):
        for side in (0, 1):
            @pl.when(has(axis, side))
            def _():
                pltpu.make_async_remote_copy(
                    src_ref=pairs[side][0], dst_ref=pairs[side][1], send_sem=send_sem.at[which, side],
                    recv_sem=recv_sem.at[which, 1 - side], device_id=beside(axis, side), device_id_type=MESH).start()
        for side in (0, 1):
            @pl.when(has(axis, side))
            def _():
                copy = pltpu.make_async_remote_copy(
                    src_ref=pairs[side][0], dst_ref=pairs[1 - side][1], send_sem=send_sem.at[which, side],
                    recv_sem=recv_sem.at[which, side], device_id=beside(axis, side), device_id_type=MESH)
                copy.wait_send()
                copy.wait_recv()

    block = lax.rem(lax.broadcasted_iota(jnp.int32, (XR, Z), 1) + RIM, Z) // (2 * RIM)
    from_after = lax.rem(lax.broadcasted_iota(jnp.int32, (XR, Z), 1), 2 * RIM) < RIM

    def exchange(buffer, parts, width, which, rx, tz, rz):
        own_planes = slice(RIM, RIM + Y)
        low, high = RIM - width, RIM + Y + width
        swap("gx", which, (
            (buffer.at[:, own_planes, 0:2 * RIM, 0:Z], rx.at[1]),
            (buffer.at[:, own_planes, X - 2 * RIM:X, 0:Z], rx.at[0])))
        upper = lax.broadcasted_iota(jnp.int32, (Y, 2 * RIM, Z), 1) < RIM
        for c in range(parts):
            buffer[c, own_planes, X:XR, 0:Z] = jnp.where(upper, rx[1, c], rx[0, c])
        swap("gy", which + 1, (
            (buffer.at[:, RIM:RIM + width, :, 0:Z], buffer.at[:, RIM + Y:high, :, 0:Z]),
            (buffer.at[:, RIM + Y - width:RIM + Y, :, 0:Z], buffer.at[:, low:RIM, :, 0:Z])))
        for c in range(parts):
            packed = jnp.zeros((XR, Z), jnp.float32)
            for y in range(low, high):
                packed = jnp.where(block == y, pltpu.roll(buffer[c, y, :, 0:Z], (2 * RIM * y) % Z, 1), packed)
            tz[c] = packed
        swap("gz", which + 2, ((tz, rz.at[1]), (tz, rz.at[0])))
        for c in range(parts):
            both = jnp.where(from_after, rz[1, c], rz[0, c])
            for y in range(low, high):
                buffer[c, y, :, Z:ZR] = pltpu.roll(both, (-2 * RIM * y) % Z, 1)

    def clear_outside(buffer, parts):
        for side, first in ((0, 0), (1, RIM + Y)):
            @pl.when(jnp.logical_not(has("gy", side)))
            def _():
                for c in range(parts):
                    buffer[c, first:first + RIM] = jnp.zeros((RIM, XR, ZR), jnp.float32)

    exchange(mom, 3, 1, 0, rx_m, tz_m, rz_m)

    @pl.loop(RIM, RIM + Y)
    def _(y):
        xp, xm = sides(mom[0, y], 0)
        zp, zm = sides(mom[2, y], 1)
        total = (xp - xm) + (mom[1, y + 1] - mom[1, y - 1]) + (zp - zm)
        src[0, y, 0:X, 0:Z] = -0.5 * total[0:X, 0:Z] / diag[y - RIM]

    exchange(src, 1, 4, 3, rx_s, tz_s, rz_s)
    w = chebyshev_weights(1.0, 0.9, SWEEPS)

    def neighbours(buffer, y):
        xp, xm = sides(buffer[0, y], 0)
        zp, zm = sides(buffer[0, y], 1)
        return xp + xm + buffer[0, y + 1] + buffer[0, y - 1] + zp + zm

    @pl.loop(1, 2 * RIM + Y - 1)
    def _(y):
        pot1[0, y] = mask[...] * ((w[0] + w[1] - w[0] * w[1]) * src[0, y] + (w[0] * w[1] / 6.0) * neighbours(src, y))

    clear_outside(pot1, 1)

    @pl.loop(2, 2 * RIM + Y - 2)
    def _(y):
        center = pot1[0, y]
        pot2[0, y] = mask[...] * (center + w[2] * (src[0, y] - center + neighbours(pot1, y) * (1.0 / 6.0)))

    clear_outside(pot2, 1)

    @pl.loop(RIM - 1, RIM + Y + 1)
    def _(y):
        center = pot2[0, y]
        xp, xm = sides(center, 0)
        zp, zm = sides(center, 1)
        m = [mom[c, y] for c in range(3)]
        grad = [xp - xm, pot2[0, y + 1] - pot2[0, y - 1], zp - zm]
        total = [m[c] - 0.5 * grad[c] for c in range(3)]
        inner = (m[0] * total[0] + m[1] * total[1] + m[2] * total[2]) / 3.0
        for number, (a, b) in enumerate(STRAIN_PAIRS):
            if a == b:
                value = MAGNETO * (m[a] * total[a] - inner)
            else:
                value = (0.5 * MAGNETO) * (m[a] * total[b] + m[b] * total[a])
            stress[number, y] = value

    for k in range(1, ny):
        peer = lax.rem(gy + k, ny)
        copy = pltpu.make_async_remote_copy(
            src_ref=stiff.at[:, pl.ds(pl.multiple_of(peer * Y, Y), Y), :],
            dst_ref=modulus.at[pl.ds(lax.rem(gy + ny - k, ny) * span, span)],
            send_sem=g_send.at[k], recv_sem=g_recv.at[k],
            device_id=device("gy", peer), device_id_type=MESH)
        copy.wait_send()
        copy.wait_recv()
    own.wait()
    for y in range(Y):
        diag[y] = 8.0 * modulus.reshape(X * Y, Z)[pl.ds(y, X, stride=Y), :]

    @pl.loop(RIM, RIM + Y)
    def _(y):
        for a in range(3):
            xp, xm = sides(stress[STRESS_AT[a, 0], y], 0)
            zp, zm = sides(stress[STRESS_AT[a, 2], y], 1)
            n = STRESS_AT[a, 1]
            force = 0.5 * ((xp - xm) + (stress[n, y + 1] - stress[n, y - 1]) + (zp - zm))[0:X, 0:Z]
            load[a, y, 0:X, 0:Z] = force.astype(jnp.bfloat16).astype(jnp.float32) / diag[y - RIM]

    exchange(load, 3, 3, 6, rx_g, tz_g, rz_g)
    v = chebyshev_weights(1.3, 1.2, SWEEPS)

    def navier(buffer, y):
        u = [buffer[c, y] for c in range(3)]
        up = [buffer[c, y + 1] for c in range(3)]
        um = [buffer[c, y - 1] for c in range(3)]
        xs = [sides(u[c], 0) for c in range(3)]
        zs = [sides(u[c], 1) for c in range(3)]
        dy = [up[c] - um[c] for c in range(3)]
        dx0 = xs[0][0] - xs[0][1]
        dz2 = zs[2][0] - zs[2][1]
        ap, am = sides(dy[1] + dz2, 0)
        bp, bm = sides(dy[0], 0)
        cp, cm = sides(dy[2], 1)
        ep, em = sides(dx0 + dy[1], 1)
        mixed = [ap - am, (bp - bm) + (cp - cm), ep - em]
        result = []
        for c in range(3):
            along = [xs[c][0] + xs[c][1], up[c] + um[c], zs[c][0] + zs[c][1]]
            rest = along[0] + along[1] + along[2] + along[c]
            result.append(8.0 * u[c] - rest - 0.25 * mixed[c])
        return u, result

    @pl.loop(2, 2 * RIM + Y - 2)
    def _(y):
        u, result = navier(load, y)
        for c in range(3):
            disp1[c, y] = mask[...] * ((v[0] + v[1]) * u[c] - (v[0] * v[1] / 8.0) * result[c])

    clear_outside(disp1, 3)

    @pl.loop(3, 2 * RIM + Y - 3)
    def _(y):
        u, result = navier(disp1, y)
        for c in range(3):
            disp2[c, y] = mask[...] * (u[c] + v[2] * (load[c, y] - 0.125 * result[c]))

    clear_outside(disp2, 3)

    for y in range(RIM, RIM + Y):
        rows = pl.ds(y - RIM, X, stride=Y)
        gradient = {}
        for c in range(3):
            u = disp2[c, y]
            xp, xm = sides(u, 0)
            zp, zm = sides(u, 1)
            gradient[c, 0] = (xp - xm)[0:X, 0:Z]
            gradient[c, 1] = (disp2[c, y + 1] - disp2[c, y - 1])[0:X, 0:Z]
            gradient[c, 2] = (zp - zm)[0:X, 0:Z]
        for number, (a, b) in enumerate(STRAIN_PAIRS):
            flat[number, rows, :] = 0.25 * (gradient[b, a] + gradient[a, b])
    for number in range(6):
        out[number] = flat[number].astype(jnp.bfloat16)


def per_device(phase, perm_scale, magnetization, stiffness):
    X, Y, Z = phase.shape
    nx, ny, nz = (lax.axis_size(axis) for axis in ("gx", "gy", "gz"))
    XR, ZR, P2 = X + 2 * RIM, 2 * Z, Y + 2 * RIM
    f32 = jnp.float32
    field = lambda parts: pltpu.VMEM((parts, P2, XR, ZR), f32)
    rx = lambda parts: pltpu.VMEM((2, parts, Y, 2 * RIM, Z), f32)
    vmem = pl.BlockSpec(memory_space=pltpu.VMEM)
    result = pl.pallas_call(
        functools.partial(kernel, (nx, ny, nz, X, Y, Z)),
        out_shape=jax.ShapeDtypeStruct((6, X * Y, Z), jnp.bfloat16),
        in_specs=[vmem] * 4,
        out_specs=vmem,
        scratch_shapes=[
            pltpu.VMEM((6, X * Y, Z), f32), pltpu.VMEM((Y, X, Z), f32),
            field(3), field(1), field(1), field(1), field(6), field(3), field(3), field(3),
            pltpu.VMEM((XR, ZR), f32), pltpu.VMEM((X, Y, Z), f32),
            rx(3), rx(1), rx(3),
            pltpu.VMEM((3, XR, Z), f32), pltpu.VMEM((1, XR, Z), f32), pltpu.VMEM((3, XR, Z), f32),
            pltpu.VMEM((2, 3, XR, Z), f32), pltpu.VMEM((2, 1, XR, Z), f32), pltpu.VMEM((2, 3, XR, Z), f32),
            pltpu.SemaphoreType.DMA((9, 2)), pltpu.SemaphoreType.DMA((9, 2)),
            pltpu.SemaphoreType.DMA((ny,)), pltpu.SemaphoreType.DMA((ny,)), pltpu.SemaphoreType.DMA,
        ],
        compiler_params=pltpu.CompilerParams(
            collective_id=0, has_side_effects=True, vmem_limit_bytes=48 * 1024 * 1024),
    )(phase.reshape(X * Y, Z), perm_scale.reshape(X * Y, Z), magnetization.reshape(3, X * Y, Z), stiffness)
    return result.reshape(6, X, Y, Z)


def solution(mesh):
    placed = (
        P("gx", "gy", "gz"),
        P("gx", "gy", "gz"),
        P(None, "gx", "gy", "gz"),
        P(("gx", "gy"), None, "gz"),
    )
    return jax.shard_map(
        per_device, mesh=mesh, in_specs=placed, out_specs=P(None, "gx", "gy", "gz"), check_vma=False
    )
```

time: 226 us -> 60.8 us (0.27)
  starting transfers between devices: 101 us -> 0 us
  waiting for transfers between devices: 73.7 us -> 0 us
  Pallas kernels: 0 us -> 54.9 us
  other arithmetic: 22.4 us -> 0 us
  blocking collectives: 13.2 us -> 0 us
  local copies, waits for them, and re-layouts: 13.2 us -> 4.73 us
    ppermute x36 -> x0, starting transfers between devices: 97.8 us -> none  [the longest x18 74.2 us: padded_2(): before = lax.ppermute(last, axis, up)]
    ppermute x36 -> x0, waiting for transfers between devices: 67.9 us -> none  [the longest x18 56.5 us: padded_2(): after = lax.ppermute(leading, axis, down)]
    pallas_call x0 -> x1, Pallas kernels: none -> 54.9 us  [per_device(): pl.pallas_call(functools.partial(kernel, (nx, ny, nz, X, Y, Z)), out_shap...]
    all_to_all x1 -> x0, blocking collectives: 13.2 us -> none  [per_device(): return lax.all_to_all(strain, 'gy', split_axis=2, concat_axis=1, tiled=True)]
    another operation x9 -> x0, other arithmetic: 7.67 us -> none  [the longest x6 5.01 us: navier(): return jnp.stack(result)]
    all_to_all x1 -> x0, waiting for transfers between devices: 5.82 us -> none  [per_device(): lax.all_to_all(force, 'gy', split_axis=1, concat_axis=2, tiled=True)]
    concatenate x10 -> x0, other arithmetic: 4.53 us -> none  [padded_2(): value = jnp.concatenate([before, value, after], axis=dim)]
    slice x19 -> x0, local copies, waits for them, and re-layouts: 4.24 us -> none  [the longest x15 2.88 us: padded_2(): last = lax.slice_in_dim(value, length - width, length, axis=dim)]
  transfers between devices with their start and end apart: 37 -> 0, of which waited for: 26 -> 0; matrix products, arithmetic and copies ran while one was open for 1% -> 0% of each run, Pallas kernels for 0% -> 0%
where the time goes in v1:
time: 60.8 us; the launch traced here: 59.6 us
  Pallas kernels  54.9 us (90%)
  local copies, waits for them, and re-layouts  4.73 us (8%)
    pallas_call x1, Pallas kernels, per_device(): pl.pallas_call(functools.partial(kernel, (nx, ny, nz, X, Y, Z)), out_shap...  54.9 us
    unnamed x9, local copies, waits for them, and re-layouts  4.73 us

profile of v1, /device:TPU:0, one launch (start us, length us, event | category | flops | bytes accessed | tf_op | source)
XLA Modules:
  0.0 59.6 jit_solution(12710323943324254195)
XLA Ops:
  0.0 0.0 copy-start
  0.0 1.0 %copy-done = bf16[3,64,8,128]{3,2,1,0:T(8,128)(2,1)S(1)} copy-done((bf16[3,64,8,128]{3,2,1,0:T(8,128)(2,1)S(1)}, bf16[3,64,8,128]{3,2,1,0:T(8,128)(2,1)}, u32[]{:S(2)}) %copy-start) | copy-done | bytes 393240
  1.0 0.0 copy-start.1
  1.0 0.9 %copy-done.1 = s32[64,8,128]{2,1,0:T(8,128)S(1)} copy-done((s32[64,8,128]{2,1,0:T(8,128)S(1)}, s32[64,8,128]{2,1,0:T(8,128)}, u32[]{:S(2)}) %copy-start.1) | copy-done | bytes 262168
  1.9 0.0 copy-start.2
  1.9 0.9 %copy-done.2 = f32[64,8,128]{2,1,0:T(8,128)S(1)} copy-done((f32[64,8,128]{2,1,0:T(8,128)S(1)}, f32[64,8,128]{2,1,0:T(8,128)}, u32[]{:S(2)}) %copy-start.2) | copy-done | bytes 262168
  2.9 0.0 copy-start.3
  2.9 0.9 %copy-done.3 = f32[32,16,128]{2,1,0:T(8,128)S(1)} copy-done((f32[32,16,128]{2,1,0:T(8,128)S(1)}, f32[32,16,128]{2,1,0:T(8,128)}, u32[]{:S(2)}) %copy-start.3) | copy-done | bytes 262168
  3.8 54.9 %shard_map.46 = bf16[6,512,128]{2,1,0:T(8,128)(2,1)S(1)} custom-call(s32[512,128]{1,0:T(8,128)S(1)} %bitcast.6, f32[512,128]{1,0:T(8,128)S(1)} %bitcast.7, bf16[3,512,128]{2,1,0:T(8,128)(2,1)S(1)} %bitcast.5, f32[32,16,128]{2,1,0:T(8,128)S(1)} %copy-done.3), custom_call_target="tpu_custom_call" | custom-call | tf_op jit(solution)/shard_map/pallas_call | solution.py:295
  58.7 0.9 %copy.6 = bf16[6,64,8,128]{3,2,1,0:T(8,128)(2,1)} copy(bf16[6,64,8,128]{3,2,1,0:T(8,128)(2,1)S(1)} %bitcast.4) | data formatting | bytes 1572864
Async XLA Ops:
  0.0 1.0 %copy-start = (bf16[3,64,8,128]{3,2,1,0:T(8,128)(2,1)S(1)}, bf16[3,64,8,128]{3,2,1,0:T(8,128)(2,1)}, u32[]{:S(2)}) copy-start(bf16[3,64,8,128]{3,2,1,0:T(8,128)(2,1)} %param.6) | copy-start | bytes 1179652
  1.0 0.9 %copy-start.1 = (s32[64,8,128]{2,1,0:T(8,128)S(1)}, s32[64,8,128]{2,1,0:T(8,128)}, u32[]{:S(2)}) copy-start(s32[64,8,128]{2,1,0:T(8,128)} %param.4) | copy-start | bytes 786436
  1.9 0.9 %copy-start.2 = (f32[64,8,128]{2,1,0:T(8,128)S(1)}, f32[64,8,128]{2,1,0:T(8,128)}, u32[]{:S(2)}) copy-start(f32[64,8,128]{2,1,0:T(8,128)} %param.5) | copy-start | bytes 786436
  2.9 0.9 %copy-start.3 = (f32[32,16,128]{2,1,0:T(8,128)S(1)}, f32[32,16,128]{2,1,0:T(8,128)}, u32[]{:S(2)}) copy-start(f32[32,16,128]{2,1,0:T(8,128)} %stiff.1) | copy-start | bytes 786436

commit v2 on v1

--- a/solution.py
+++ b/solution.py
@@ -32,14 +32,19 @@
     return shift(value, dimension, 1), shift(value, dimension, -1)
 
 
-def kernel(sizes, phase, perm, magnet, stiff, out, flat, diag, mom, src, pot1, pot2, stress, load, disp1, disp2,
-           mask, modulus, rx_m, rx_s, rx_g, tz_m, tz_s, tz_g, rz_m, rz_s, rz_g, send_sem, recv_sem, g_send, g_recv, g_local):
+def kernel(sizes, phase_in, perm_in, magnet_in, stiff, out, phase, perm, magnet, in_sem, flat, diag, mom, src, pot1, pot2, stress, load, disp1, disp2,
+           mask, modulus, rx_m, rx_s, rx_g, tz_a, tz_m, tz_s, tz_g, rz_a, rz_m, rz_s, rz_g, send_sem, recv_sem, g_send, g_recv, g_local):
     nx, ny, nz, X, Y, Z = sizes
     XR, ZR = X + 2 * RIM, 2 * Z
     gx, gy, gz = lax.axis_index("gx"), lax.axis_index("gy"), lax.axis_index("gz")
     place = {"gx": gx, "gy": gy, "gz": gz}
     count = {"gx": nx, "gy": ny, "gz": nz}
 
+    fetches = [pltpu.make_async_copy(a, b, in_sem.at[i]) for i, (a, b) in enumerate(
+        ((magnet_in, magnet), (phase_in, phase), (perm_in, perm)))]
+    for fetch in fetches:
+        fetch.start()
+
     def has(axis, side):
         return place[axis] > 0 if side == 0 else place[axis] < count[axis] - 1
 
@@ -48,20 +53,37 @@
         at[axis] = index
         return (at["gx"], at["gy"], at["gz"])
 
-    def beside(axis, side):
-        return device(axis, place[axis] + (-1 if side == 0 else 1))
+    def exists(step):
+        there = None
+        for axis, move in zip(("gx", "gy", "gz"), step):
+            if move:
+                this = has(axis, 0 if move < 0 else 1)
+                there = this if there is None else there & this
+        return there
+
+    def beside(step):
+        return (gx + step[0], gy + step[1], gz + step[2])
 
     barrier = pltpu.get_barrier_semaphore()
     greeted = 0
-    for axis in ("gx", "gz"):
-        for side in (0, 1):
-            @pl.when(has(axis, side))
-            def _():
-                pl.semaphore_signal(barrier, inc=1, device_id=beside(axis, side), device_id_type=MESH)
-            greeted = greeted + has(axis, side).astype(jnp.int32)
+    diagonals = [(dx, dy, 0) for dx in (-1, 1) for dy in (-1, 1)]
+    for step in [(-1, 0, 0), (1, 0, 0), (0, 0, -1), (0, 0, 1)] + diagonals:
+        @pl.when(exists(step))
+        def _():
+            pl.semaphore_signal(barrier, inc=1, device_id=beside(step), device_id_type=MESH)
+        greeted = greeted + exists(step).astype(jnp.int32)
     for k in range(1, ny):
         pl.semaphore_signal(barrier, inc=1, device_id=device("gy", lax.rem(gy + k, ny)), device_id_type=MESH)
     greeted = greeted + (ny - 1)
+
+    row = lax.broadcasted_iota(jnp.int32, (XR, ZR), 0)
+    lane = lax.broadcasted_iota(jnp.int32, (XR, ZR), 1)
+    real = ((row < X) | ((row < X + RIM) & has("gx", 1)) | ((row >= X + RIM) & has("gx", 0))) & (
+        (lane < Z) | ((lane < Z + Z // 2) & has("gz", 1)) | ((lane >= Z + Z // 2) & has("gz", 0)))
+    mask[...] = jnp.where(real, 1.0, 0.0)
+
+    for fetch in fetches:
+        fetch.wait()
 
     for c in range(3):
         flat[c] = magnet[c].astype(jnp.float32)
@@ -74,18 +96,19 @@
         for c in range(3):
             mom[c, RIM + y, 0:X, 0:Z] = jnp.where(magnetic, flat[c, rows, :], 0.0)
 
-    row = lax.broadcasted_iota(jnp.int32, (XR, ZR), 0)
-    lane = lax.broadcasted_iota(jnp.int32, (XR, ZR), 1)
-    real = ((row < X) | ((row < X + RIM) & has("gx", 1)) | ((row >= X + RIM) & has("gx", 0))) & (
-        (lane < Z) | ((lane < Z + Z // 2) & has("gz", 1)) | ((lane >= Z + Z // 2) & has("gz", 0)))
-    mask[...] = jnp.where(real, 1.0, 0.0)
-
     for buffer in (rx_m, rx_s, rx_g):
         for side in (0, 1):
             @pl.when(jnp.logical_not(has("gx", side)))
             def _():
                 buffer[side] = jnp.zeros(buffer.shape[1:], jnp.float32)
-    for buffer in (rz_m, rz_s, rz_g):
+    for buffer in (rx_m, rx_s, rx_g):
+        for side, first in ((0, 0), (1, RIM + Y)):
+            @pl.when(jnp.logical_not(has("gy", side)))
+            def _():
+                for way in (0, 1):
+                    for c in range(buffer.shape[1]):
+                        buffer[way, c, first:first + RIM] = jnp.zeros((RIM, 2 * RIM, Z), jnp.float32)
+    for buffer in (rz_a, rz_m, rz_s, rz_g):
         for side in (0, 1):
             @pl.when(jnp.logical_not(has("gz", side)))
             def _():
@@ -98,6 +121,101 @@
                     buffer[c, first:first + RIM] = jnp.zeros((RIM, XR, ZR), jnp.float32)
 
     pl.semaphore_wait(barrier, greeted)
+
+    def copy_of(piece, number):
+        step, source, target = piece
+        return pltpu.make_async_remote_copy(
+            src_ref=source, dst_ref=target, send_sem=send_sem.at[number], recv_sem=recv_sem.at[number],
+            device_id=beside(step), device_id_type=MESH)
+
+    def begin(pieces, base):
+        for number, piece in enumerate(pieces):
+            @pl.when(exists(piece[0]))
+            def _():
+                copy_of(piece, base + number).start()
+
+    def finish(pieces, base):
+        for number, piece in enumerate(pieces):
+            @pl.when(exists(piece[0]))
+            def _():
+                copy_of(piece, base + number).wait_send()
+            @pl.when(exists([-move for move in piece[0]]))
+            def _():
+                copy_of(piece, base + number).wait_recv()
+
+    def flat_pieces(buffer, width, rx):
+        planes = {-1: slice(RIM, RIM + width), 0: slice(RIM, RIM + Y), 1: slice(RIM + Y - width, RIM + Y)}
+        landing = {-1: slice(RIM + Y, RIM + Y + width), 0: slice(RIM, RIM + Y), 1: slice(RIM - width, RIM)}
+        rows = {-1: slice(0, 2 * RIM), 1: slice(X - 2 * RIM, X)}
+        pieces = []
+        for dy in (-1, 1):
+            pieces.append(((0, dy, 0), buffer.at[:, planes[dy], 0:X, 0:Z], buffer.at[:, landing[dy], 0:X, 0:Z]))
+        for dy in (0, -1, 1):
+            for dx in (-1, 1):
+                pieces.append(((dx, dy, 0), buffer.at[:, planes[dy], rows[dx], 0:Z],
+                               rx.at[1 if dx < 0 else 0, :, landing[dy]]))
+        return pieces
+
+    def place_rows(buffer, parts, width, rx):
+        upper = lax.broadcasted_iota(jnp.int32, (Y + 2 * width, 2 * RIM, Z), 1) < RIM
+        span = slice(RIM - width, RIM + Y + width)
+        for c in range(parts):
+            buffer[c, span, X:XR, 0:Z] = jnp.where(upper, rx[1, c, span], rx[0, c, span])
+
+    block = lax.rem(lax.broadcasted_iota(jnp.int32, (XR, Z), 1) + RIM, Z) // (2 * RIM)
+    from_after = lax.rem(lax.broadcasted_iota(jnp.int32, (XR, Z), 1), 2 * RIM) < RIM
+
+    def pack(buffer, components, width, rows, tz):
+        for at, c in enumerate(components):
+            packed = jnp.zeros((rows, Z), jnp.float32)
+            for y in range(RIM - width, RIM + Y + width):
+                packed = jnp.where(
+                    block[0:rows] == y, pltpu.roll(buffer[c, y, 0:rows, 0:Z], (2 * RIM * y) % Z, 1), packed)
+            tz[at] = packed
+
+    def unpack(buffer, components, width, rows, rz):
+        for at, c in enumerate(components):
+            both = jnp.where(from_after[0:rows], rz[1, at], rz[0, at])
+            for y in range(RIM - width, RIM + Y + width):
+                buffer[c, y, 0:rows, Z:ZR] = pltpu.roll(both, (-2 * RIM * y) % Z, 1)
+
+    def deep_pieces(tz, rz):
+        return [((0, 0, -1), tz, rz.at[1]), ((0, 0, 1), tz, rz.at[0])]
+
+    def clear_outside(buffer, parts):
+        for side, first in ((0, 0), (1, RIM + Y)):
+            @pl.when(jnp.logical_not(has("gy", side)))
+            def _():
+                for c in range(parts):
+                    buffer[c, first:first + RIM] = jnp.zeros((RIM, XR, ZR), jnp.float32)
+
+    flat_m = flat_pieces(mom, 1, rx_m)
+    deep_a = deep_pieces(tz_a, rz_a)
+    begin(flat_m, 0)
+    pack(mom, (2,), 0, X, tz_a)
+    begin(deep_a, 8)
+    finish(flat_m, 0)
+    place_rows(mom, 3, 1, rx_m)
+    finish(deep_a, 8)
+    unpack(mom, (2,), 0, X, rz_a)
+
+    @pl.loop(RIM, RIM + Y)
+    def _(y):
+        xp, xm = sides(mom[0, y], 0)
+        zp, zm = sides(mom[2, y], 1)
+        total = (xp - xm) + (mom[1, y + 1] - mom[1, y - 1]) + (zp - zm)
+        src[0, y, 0:X, 0:Z] = -0.5 * total[0:X, 0:Z] / diag[y - RIM]
+
+    flat_s = flat_pieces(src, 4, rx_s)
+    deep_s = deep_pieces(tz_s, rz_s)
+    deep_m = deep_pieces(tz_m, rz_m)
+    begin(flat_s, 10)
+    pack(mom, (0, 1, 2), 1, XR, tz_m)
+    begin(deep_m, 18)
+    finish(flat_s, 10)
+    place_rows(src, 1, 4, rx_s)
+    pack(src, (0,), 4, XR, tz_s)
+    begin(deep_s, 20)
 
     span = X // ny
     for k in range(1, ny):
@@ -111,65 +229,8 @@
         stiff.at[:, pl.ds(pl.multiple_of(gy * Y, Y), Y), :], modulus.at[pl.ds(gy * span, span)], g_local)
     own.start()
 
-    def swap(axis, which, pairs):
-        for side in (0, 1):
-            @pl.when(has(axis, side))
-            def _():
-                pltpu.make_async_remote_copy(
-                    src_ref=pairs[side][0], dst_ref=pairs[side][1], send_sem=send_sem.at[which, side],
-                    recv_sem=recv_sem.at[which, 1 - side], device_id=beside(axis, side), device_id_type=MESH).start()
-        for side in (0, 1):
-            @pl.when(has(axis, side))
-            def _():
-                copy = pltpu.make_async_remote_copy(
-                    src_ref=pairs[side][0], dst_ref=pairs[1 - side][1], send_sem=send_sem.at[which, side],
-                    recv_sem=recv_sem.at[which, side], device_id=beside(axis, side), device_id_type=MESH)
-                copy.wait_send()
-                copy.wait_recv()
-
-    block = lax.rem(lax.broadcasted_iota(jnp.int32, (XR, Z), 1) + RIM, Z) // (2 * RIM)
-    from_after = lax.rem(lax.broadcasted_iota(jnp.int32, (XR, Z), 1), 2 * RIM) < RIM
-
-    def exchange(buffer, parts, width, which, rx, tz, rz):
-        own_planes = slice(RIM, RIM + Y)
-        low, high = RIM - width, RIM + Y + width
-        swap("gx", which, (
-            (buffer.at[:, own_planes, 0:2 * RIM, 0:Z], rx.at[1]),
-            (buffer.at[:, own_planes, X - 2 * RIM:X, 0:Z], rx.at[0])))
-        upper = lax.broadcasted_iota(jnp.int32, (Y, 2 * RIM, Z), 1) < RIM
-        for c in range(parts):
-            buffer[c, own_planes, X:XR, 0:Z] = jnp.where(upper, rx[1, c], rx[0, c])
-        swap("gy", which + 1, (
-            (buffer.at[:, RIM:RIM + width, :, 0:Z], buffer.at[:, RIM + Y:high, :, 0:Z]),
-            (buffer.at[:, RIM + Y - width:RIM + Y, :, 0:Z], buffer.at[:, low:RIM, :, 0:Z])))
-        for c in range(parts):
-            packed = jnp.zeros((XR, Z), jnp.float32)
-            for y in range(low, high):
-                packed = jnp.where(block == y, pltpu.roll(buffer[c, y, :, 0:Z], (2 * RIM * y) % Z, 1), packed)
-            tz[c] = packed
-        swap("gz", which + 2, ((tz, rz.at[1]), (tz, rz.at[0])))
-        for c in range(parts):
-            both = jnp.where(from_after, rz[1, c], rz[0, c])
-            for y in range(low, high):
-                buffer[c, y, :, Z:ZR] = pltpu.roll(both, (-2 * RIM * y) % Z, 1)
-
-    def clear_outside(buffer, parts):
-        for side, first in ((0, 0), (1, RIM + Y)):
-            @pl.when(jnp.logical_not(has("gy", side)))
-            def _():
-                for c in range(parts):
-                    buffer[c, first:first + RIM] = jnp.zeros((RIM, XR, ZR), jnp.float32)
-
-    exchange(mom, 3, 1, 0, rx_m, tz_m, rz_m)
-
-    @pl.loop(RIM, RIM + Y)
-    def _(y):
-        xp, xm = sides(mom[0, y], 0)
-        zp, zm = sides(mom[2, y], 1)
-        total = (xp - xm) + (mom[1, y + 1] - mom[1, y - 1]) + (zp - zm)
-        src[0, y, 0:X, 0:Z] = -0.5 * total[0:X, 0:Z] / diag[y - RIM]
-
-    exchange(src, 1, 4, 3, rx_s, tz_s, rz_s)
+    finish(deep_s, 20)
+    unpack(src, (0,), 4, XR, rz_s)
     w = chebyshev_weights(1.0, 0.9, SWEEPS)
 
     def neighbours(buffer, y):
@@ -189,6 +250,9 @@
         pot2[0, y] = mask[...] * (center + w[2] * (src[0, y] - center + neighbours(pot1, y) * (1.0 / 6.0)))
 
     clear_outside(pot2, 1)
+
+    finish(deep_m, 18)
+    unpack(mom, (0, 1, 2), 1, XR, rz_m)
 
     @pl.loop(RIM - 1, RIM + Y + 1)
     def _(y):
@@ -228,7 +292,15 @@
             force = 0.5 * ((xp - xm) + (stress[n, y + 1] - stress[n, y - 1]) + (zp - zm))[0:X, 0:Z]
             load[a, y, 0:X, 0:Z] = force.astype(jnp.bfloat16).astype(jnp.float32) / diag[y - RIM]
 
-    exchange(load, 3, 3, 6, rx_g, tz_g, rz_g)
+    flat_g = flat_pieces(load, 3, rx_g)
+    deep_g = deep_pieces(tz_g, rz_g)
+    begin(flat_g, 22)
+    finish(flat_g, 22)
+    place_rows(load, 3, 3, rx_g)
+    pack(load, (0, 1, 2), 3, XR, tz_g)
+    begin(deep_g, 30)
+    finish(deep_g, 30)
+    unpack(load, (0, 1, 2), 3, XR, rz_g)
     v = chebyshev_weights(1.3, 1.2, SWEEPS)
 
     def navier(buffer, y):
@@ -290,25 +362,27 @@
     XR, ZR, P2 = X + 2 * RIM, 2 * Z, Y + 2 * RIM
     f32 = jnp.float32
     field = lambda parts: pltpu.VMEM((parts, P2, XR, ZR), f32)
-    rx = lambda parts: pltpu.VMEM((2, parts, Y, 2 * RIM, Z), f32)
+    rx = lambda parts: pltpu.VMEM((2, parts, P2, 2 * RIM, Z), f32)
     vmem = pl.BlockSpec(memory_space=pltpu.VMEM)
     result = pl.pallas_call(
         functools.partial(kernel, (nx, ny, nz, X, Y, Z)),
         out_shape=jax.ShapeDtypeStruct((6, X * Y, Z), jnp.bfloat16),
-        in_specs=[vmem] * 4,
+        in_specs=[pl.BlockSpec(memory_space=pl.ANY)] * 4,
         out_specs=vmem,
         scratch_shapes=[
+            pltpu.VMEM((X * Y, Z), jnp.int32), pltpu.VMEM((X * Y, Z), f32), pltpu.VMEM((3, X * Y, Z), jnp.bfloat16),
+            pltpu.SemaphoreType.DMA((3,)),
             pltpu.VMEM((6, X * Y, Z), f32), pltpu.VMEM((Y, X, Z), f32),
             field(3), field(1), field(1), field(1), field(6), field(3), field(3), field(3),
             pltpu.VMEM((XR, ZR), f32), pltpu.VMEM((X, Y, Z), f32),
             rx(3), rx(1), rx(3),
-            pltpu.VMEM((3, XR, Z), f32), pltpu.VMEM((1, XR, Z), f32), pltpu.VMEM((3, XR, Z), f32),
-            pltpu.VMEM((2, 3, XR, Z), f32), pltpu.VMEM((2, 1, XR, Z), f32), pltpu.VMEM((2, 3, XR, Z), f32),
-            pltpu.SemaphoreType.DMA((9, 2)), pltpu.SemaphoreType.DMA((9, 2)),
+            pltpu.VMEM((1, X, Z), f32), pltpu.VMEM((3, XR, Z), f32), pltpu.VMEM((1, XR, Z), f32), pltpu.VMEM((3, XR, Z), f32),
+            pltpu.VMEM((2, 1, X, Z), f32), pltpu.VMEM((2, 3, XR, Z), f32), pltpu.VMEM((2, 1, XR, Z), f32), pltpu.VMEM((2, 3, XR, Z), f32),
+            pltpu.SemaphoreType.DMA((32,)), pltpu.SemaphoreType.DMA((32,)),
             pltpu.SemaphoreType.DMA((ny,)), pltpu.SemaphoreType.DMA((ny,)), pltpu.SemaphoreType.DMA,
         ],
         compiler_params=pltpu.CompilerParams(
-            collective_id=0, has_side_effects=True, vmem_limit_bytes=48 * 1024 * 1024),
+            collective_id=0, has_side_effects=True, vmem_limit_bytes=60 * 1024 * 1024),
     )(phase.reshape(X * Y, Z), perm_scale.reshape(X * Y, Z), magnetization.reshape(3, X * Y, Z), stiffness)
     return result.reshape(6, X, Y, Z)
 

time: 60.8 us -> 51.5 us (0.85); the launches traced: 59.6 us -> 51.3 us
  Pallas kernels: 54.9 us -> 49.3 us
  local copies, waits for them, and re-layouts: 4.73 us -> 2.06 us
    pallas_call x1, Pallas kernels: 54.9 us -> 49.3 us  [per_device(): pl.pallas_call(functools.partial(kernel, (nx, ny, nz, X, Y, Z)), out_shap...]
    unnamed x9 -> x1, local copies, waits for them, and re-layouts: 4.73 us -> 2.06 us
where the time goes in v2:
time: 51.5 us; the launch traced here: 51.3 us
  Pallas kernels  49.3 us (96%)
  local copies, waits for them, and re-layouts  2.06 us (4%)
    pallas_call x1, Pallas kernels, per_device(): pl.pallas_call(functools.partial(kernel, (nx, ny, nz, X, Y, Z)), out_shap...  49.3 us
    unnamed x1, local copies, waits for them, and re-layouts  2.06 us

profile of v2, /device:TPU:0, one launch (start us, length us, event | category | flops | bytes accessed | tf_op | source)
XLA Modules:
  0.0 51.3 jit_solution(6811287483961846922)
XLA Ops:
  0.0 49.3 %shard_map.46 = bf16[6,512,128]{2,1,0:T(8,128)(2,1)} custom-call(s32[512,128]{1,0:T(8,128)} %bitcast.6, f32[512,128]{1,0:T(8,128)} %bitcast.7, bf16[3,512,128]{2,1,0:T(8,128)(2,1)} %bitcast.5, f32[32,16,128]{2,1,0:T(8,128)} %stiff.1), custom_call_target="tpu_custom_call" | custom-call | tf_op jit(solution)/shard_map/pallas_call | solution.py:367
  49.3 2.1 %copy.6 = bf16[6,64,8,128]{3,2,1,0:T(8,128)(2,1)} copy(bf16[6,64,8,128]{3,2,1,0:T(8,128)(2,1)} %bitcast.4) | data formatting | bytes 1572864

commit v3 on v2

--- a/solution.py
+++ b/solution.py
@@ -143,44 +143,44 @@
             def _():
                 copy_of(piece, base + number).wait_recv()
 
-    def flat_pieces(buffer, width, rx):
+    def flat_pieces(buffer, width, rx, parts=slice(None)):
         planes = {-1: slice(RIM, RIM + width), 0: slice(RIM, RIM + Y), 1: slice(RIM + Y - width, RIM + Y)}
         landing = {-1: slice(RIM + Y, RIM + Y + width), 0: slice(RIM, RIM + Y), 1: slice(RIM - width, RIM)}
         rows = {-1: slice(0, 2 * RIM), 1: slice(X - 2 * RIM, X)}
         pieces = []
         for dy in (-1, 1):
-            pieces.append(((0, dy, 0), buffer.at[:, planes[dy], 0:X, 0:Z], buffer.at[:, landing[dy], 0:X, 0:Z]))
+            pieces.append(((0, dy, 0), buffer.at[parts, planes[dy], 0:X, 0:Z], buffer.at[parts, landing[dy], 0:X, 0:Z]))
         for dy in (0, -1, 1):
             for dx in (-1, 1):
-                pieces.append(((dx, dy, 0), buffer.at[:, planes[dy], rows[dx], 0:Z],
-                               rx.at[1 if dx < 0 else 0, :, landing[dy]]))
+                pieces.append(((dx, dy, 0), buffer.at[parts, planes[dy], rows[dx], 0:Z],
+                               rx.at[1 if dx < 0 else 0, parts, landing[dy]]))
         return pieces
 
-    def place_rows(buffer, parts, width, rx):
+    def place_rows(buffer, components, width, rx):
         upper = lax.broadcasted_iota(jnp.int32, (Y + 2 * width, 2 * RIM, Z), 1) < RIM
         span = slice(RIM - width, RIM + Y + width)
-        for c in range(parts):
+        for c in components:
             buffer[c, span, X:XR, 0:Z] = jnp.where(upper, rx[1, c, span], rx[0, c, span])
 
     block = lax.rem(lax.broadcasted_iota(jnp.int32, (XR, Z), 1) + RIM, Z) // (2 * RIM)
     from_after = lax.rem(lax.broadcasted_iota(jnp.int32, (XR, Z), 1), 2 * RIM) < RIM
 
-    def pack(buffer, components, width, rows, tz):
-        for at, c in enumerate(components):
+    def pack(buffer, components, width, rows, tz, first=0):
+        for at, c in enumerate(components, first):
             packed = jnp.zeros((rows, Z), jnp.float32)
             for y in range(RIM - width, RIM + Y + width):
                 packed = jnp.where(
                     block[0:rows] == y, pltpu.roll(buffer[c, y, 0:rows, 0:Z], (2 * RIM * y) % Z, 1), packed)
             tz[at] = packed
 
-    def unpack(buffer, components, width, rows, rz):
-        for at, c in enumerate(components):
+    def unpack(buffer, components, width, rows, rz, first=0):
+        for at, c in enumerate(components, first):
             both = jnp.where(from_after[0:rows], rz[1, at], rz[0, at])
             for y in range(RIM - width, RIM + Y + width):
                 buffer[c, y, 0:rows, Z:ZR] = pltpu.roll(both, (-2 * RIM * y) % Z, 1)
 
-    def deep_pieces(tz, rz):
-        return [((0, 0, -1), tz, rz.at[1]), ((0, 0, 1), tz, rz.at[0])]
+    def deep_pieces(tz, rz, parts=slice(None)):
+        return [((0, 0, -1), tz.at[parts], rz.at[1, parts]), ((0, 0, 1), tz.at[parts], rz.at[0, parts])]
 
     def clear_outside(buffer, parts):
         for side, first in ((0, 0), (1, RIM + Y)):
@@ -195,7 +195,7 @@
     pack(mom, (2,), 0, X, tz_a)
     begin(deep_a, 8)
     finish(flat_m, 0)
-    place_rows(mom, 3, 1, rx_m)
+    place_rows(mom, (0, 1, 2), 1, rx_m)
     finish(deep_a, 8)
     unpack(mom, (2,), 0, X, rz_a)
 
@@ -213,7 +213,7 @@
     pack(mom, (0, 1, 2), 1, XR, tz_m)
     begin(deep_m, 18)
     finish(flat_s, 10)
-    place_rows(src, 1, 4, rx_s)
+    place_rows(src, (0,), 4, rx_s)
     pack(src, (0,), 4, XR, tz_s)
     begin(deep_s, 20)
 
@@ -283,24 +283,26 @@
     for y in range(Y):
         diag[y] = 8.0 * modulus.reshape(X * Y, Z)[pl.ds(y, X, stride=Y), :]
 
-    @pl.loop(RIM, RIM + Y)
-    def _(y):
-        for a in range(3):
+    flat_g = [flat_pieces(load, 3, rx_g, slice(a, a + 1)) for a in range(3)]
+    deep_g = [deep_pieces(tz_g, rz_g, slice(a, a + 1)) for a in range(3)]
+    for a in range(3):
+        @pl.loop(RIM, RIM + Y)
+        def _(y):
             xp, xm = sides(stress[STRESS_AT[a, 0], y], 0)
             zp, zm = sides(stress[STRESS_AT[a, 2], y], 1)
             n = STRESS_AT[a, 1]
             force = 0.5 * ((xp - xm) + (stress[n, y + 1] - stress[n, y - 1]) + (zp - zm))[0:X, 0:Z]
             load[a, y, 0:X, 0:Z] = force.astype(jnp.bfloat16).astype(jnp.float32) / diag[y - RIM]
 
-    flat_g = flat_pieces(load, 3, rx_g)
-    deep_g = deep_pieces(tz_g, rz_g)
-    begin(flat_g, 22)
-    finish(flat_g, 22)
-    place_rows(load, 3, 3, rx_g)
-    pack(load, (0, 1, 2), 3, XR, tz_g)
-    begin(deep_g, 30)
-    finish(deep_g, 30)
-    unpack(load, (0, 1, 2), 3, XR, rz_g)
+        begin(flat_g[a], 22 + 10 * a)
+    for a in range(3):
+        finish(flat_g[a], 22 + 10 * a)
+        place_rows(load, (a,), 3, rx_g)
+        pack(load, (a,), 3, XR, tz_g, a)
+        begin(deep_g[a], 30 + 10 * a)
+    for a in range(3):
+        finish(deep_g[a], 30 + 10 * a)
+        unpack(load, (a,), 3, XR, rz_g, a)
     v = chebyshev_weights(1.3, 1.2, SWEEPS)
 
     def navier(buffer, y):
@@ -378,7 +380,7 @@
             rx(3), rx(1), rx(3),
             pltpu.VMEM((1, X, Z), f32), pltpu.VMEM((3, XR, Z), f32), pltpu.VMEM((1, XR, Z), f32), pltpu.VMEM((3, XR, Z), f32),
             pltpu.VMEM((2, 1, X, Z), f32), pltpu.VMEM((2, 3, XR, Z), f32), pltpu.VMEM((2, 1, XR, Z), f32), pltpu.VMEM((2, 3, XR, Z), f32),
-            pltpu.SemaphoreType.DMA((32,)), pltpu.SemaphoreType.DMA((32,)),
+            pltpu.SemaphoreType.DMA((52,)), pltpu.SemaphoreType.DMA((52,)),
             pltpu.SemaphoreType.DMA((ny,)), pltpu.SemaphoreType.DMA((ny,)), pltpu.SemaphoreType.DMA,
         ],
         compiler_params=pltpu.CompilerParams(

time: 51.5 us -> 49.7 us (0.965)
  Pallas kernels: 49.3 us -> 47.5 us
    pallas_call x1, Pallas kernels: 49.3 us -> 47.5 us  [per_device(): pl.pallas_call(functools.partial(kernel, (nx, ny, nz, X, Y, Z)), out_shap...]
where the time goes in v3:
time: 49.7 us; the launch traced here: 49.6 us
  Pallas kernels  47.5 us (96%)
  local copies, waits for them, and re-layouts  2.06 us (4%)
    pallas_call x1, Pallas kernels, per_device(): pl.pallas_call(functools.partial(kernel, (nx, ny, nz, X, Y, Z)), out_shap...  47.5 us
    unnamed x1, local copies, waits for them, and re-layouts  2.06 us

profile of v3, /device:TPU:0, one launch (start us, length us, event | category | flops | bytes accessed | tf_op | source)
XLA Modules:
  0.0 49.6 jit_solution(15832976186122666107)
XLA Ops:
  0.0 47.5 %shard_map.46 = bf16[6,512,128]{2,1,0:T(8,128)(2,1)} custom-call(s32[512,128]{1,0:T(8,128)} %bitcast.6, f32[512,128]{1,0:T(8,128)} %bitcast.7, bf16[3,512,128]{2,1,0:T(8,128)(2,1)} %bitcast.5, f32[32,16,128]{2,1,0:T(8,128)} %stiff.1), custom_call_target="tpu_custom_call" | custom-call | tf_op jit(solution)/shard_map/pallas_call | solution.py:369
  47.5 2.1 %copy.6 = bf16[6,64,8,128]{3,2,1,0:T(8,128)(2,1)} copy(bf16[6,64,8,128]{3,2,1,0:T(8,128)(2,1)} %bitcast.4) | data formatting | bytes 1572864

commit v4 on v3

--- a/solution.py
+++ b/solution.py
@@ -199,7 +199,7 @@
     finish(deep_a, 8)
     unpack(mom, (2,), 0, X, rz_a)
 
-    @pl.loop(RIM, RIM + Y)
+    @pl.loop(RIM, RIM + Y, unroll=2)
     def _(y):
         xp, xm = sides(mom[0, y], 0)
         zp, zm = sides(mom[2, y], 1)
@@ -238,13 +238,13 @@
         zp, zm = sides(buffer[0, y], 1)
         return xp + xm + buffer[0, y + 1] + buffer[0, y - 1] + zp + zm
 
-    @pl.loop(1, 2 * RIM + Y - 1)
+    @pl.loop(1, 2 * RIM + Y - 1, unroll=2)
     def _(y):
         pot1[0, y] = mask[...] * ((w[0] + w[1] - w[0] * w[1]) * src[0, y] + (w[0] * w[1] / 6.0) * neighbours(src, y))
 
     clear_outside(pot1, 1)
 
-    @pl.loop(2, 2 * RIM + Y - 2)
+    @pl.loop(2, 2 * RIM + Y - 2, unroll=2)
     def _(y):
         center = pot1[0, y]
         pot2[0, y] = mask[...] * (center + w[2] * (src[0, y] - center + neighbours(pot1, y) * (1.0 / 6.0)))
@@ -254,7 +254,7 @@
     finish(deep_m, 18)
     unpack(mom, (0, 1, 2), 1, XR, rz_m)
 
-    @pl.loop(RIM - 1, RIM + Y + 1)
+    @pl.loop(RIM - 1, RIM + Y + 1, unroll=2)
     def _(y):
         center = pot2[0, y]
         xp, xm = sides(center, 0)
@@ -286,7 +286,7 @@
     flat_g = [flat_pieces(load, 3, rx_g, slice(a, a + 1)) for a in range(3)]
     deep_g = [deep_pieces(tz_g, rz_g, slice(a, a + 1)) for a in range(3)]
     for a in range(3):
-        @pl.loop(RIM, RIM + Y)
+        @pl.loop(RIM, RIM + Y, unroll=2)
         def _(y):
             xp, xm = sides(stress[STRESS_AT[a, 0], y], 0)
             zp, zm = sides(stress[STRESS_AT[a, 2], y], 1)
@@ -326,7 +326,7 @@
             result.append(8.0 * u[c] - rest - 0.25 * mixed[c])
         return u, result
 
-    @pl.loop(2, 2 * RIM + Y - 2)
+    @pl.loop(2, 2 * RIM + Y - 2, unroll=2)
     def _(y):
         u, result = navier(load, y)
         for c in range(3):
@@ -334,7 +334,7 @@
 
     clear_outside(disp1, 3)
 
-    @pl.loop(3, 2 * RIM + Y - 3)
+    @pl.loop(3, 2 * RIM + Y - 3, unroll=2)
     def _(y):
         u, result = navier(disp1, y)
         for c in range(3):

time: 49.7 us -> 46.6 us (0.938)
  Pallas kernels: 47.5 us -> 44.4 us
    pallas_call x1, Pallas kernels: 47.5 us -> 44.4 us  [per_device(): pl.pallas_call(functools.partial(kernel, (nx, ny, nz, X, Y, Z)), out_shap...]
where the time goes in v4:
time: 46.6 us; the launch traced here: 46.4 us
  Pallas kernels  44.4 us (95%)
  local copies, waits for them, and re-layouts  2.06 us (4%)
    pallas_call x1, Pallas kernels, per_device(): pl.pallas_call(functools.partial(kernel, (nx, ny, nz, X, Y, Z)), out_shap...  44.4 us
    unnamed x1, local copies, waits for them, and re-layouts  2.06 us

profile of v4, /device:TPU:0, one launch (start us, length us, event | category | flops | bytes accessed | tf_op | source)
XLA Modules:
  0.0 46.4 jit_solution(13540715898248873645)
XLA Ops:
  0.0 44.4 %shard_map.46 = bf16[6,512,128]{2,1,0:T(8,128)(2,1)} custom-call(s32[512,128]{1,0:T(8,128)} %bitcast.6, f32[512,128]{1,0:T(8,128)} %bitcast.7, bf16[3,512,128]{2,1,0:T(8,128)(2,1)} %bitcast.5, f32[32,16,128]{2,1,0:T(8,128)} %stiff.1), custom_call_target="tpu_custom_call" | custom-call | tf_op jit(solution)/shard_map/pallas_call | solution.py:369
  44.4 2.1 %copy.6 = bf16[6,64,8,128]{3,2,1,0:T(8,128)(2,1)} copy(bf16[6,64,8,128]{3,2,1,0:T(8,128)(2,1)} %bitcast.4) | data formatting | bytes 1572864

commit v5 on v4

--- a/solution.py
+++ b/solution.py
@@ -199,7 +199,7 @@
     finish(deep_a, 8)
     unpack(mom, (2,), 0, X, rz_a)
 
-    @pl.loop(RIM, RIM + Y, unroll=2)
+    @pl.loop(RIM, RIM + Y, unroll=4)
     def _(y):
         xp, xm = sides(mom[0, y], 0)
         zp, zm = sides(mom[2, y], 1)
@@ -244,7 +244,7 @@
 
     clear_outside(pot1, 1)
 
-    @pl.loop(2, 2 * RIM + Y - 2, unroll=2)
+    @pl.loop(2, 2 * RIM + Y - 2, unroll=4)
     def _(y):
         center = pot1[0, y]
         pot2[0, y] = mask[...] * (center + w[2] * (src[0, y] - center + neighbours(pot1, y) * (1.0 / 6.0)))
@@ -286,7 +286,7 @@
     flat_g = [flat_pieces(load, 3, rx_g, slice(a, a + 1)) for a in range(3)]
     deep_g = [deep_pieces(tz_g, rz_g, slice(a, a + 1)) for a in range(3)]
     for a in range(3):
-        @pl.loop(RIM, RIM + Y, unroll=2)
+        @pl.loop(RIM, RIM + Y, unroll=4)
         def _(y):
             xp, xm = sides(stress[STRESS_AT[a, 0], y], 0)
             zp, zm = sides(stress[STRESS_AT[a, 2], y], 1)
@@ -326,7 +326,7 @@
             result.append(8.0 * u[c] - rest - 0.25 * mixed[c])
         return u, result
 
-    @pl.loop(2, 2 * RIM + Y - 2, unroll=2)
+    @pl.loop(2, 2 * RIM + Y - 2, unroll=4)
     def _(y):
         u, result = navier(load, y)
         for c in range(3):

time: 46.6 us -> 45.7 us (0.981)
  Pallas kernels: 44.4 us -> 43.5 us
    pallas_call x1, Pallas kernels: 44.4 us -> 43.5 us  [per_device(): pl.pallas_call(functools.partial(kernel, (nx, ny, nz, X, Y, Z)), out_shap...]
where the time goes in v5:
time: 45.7 us; the launch traced here: 45.5 us
  Pallas kernels  43.5 us (95%)
  local copies, waits for them, and re-layouts  2.06 us (5%)
    pallas_call x1, Pallas kernels, per_device(): pl.pallas_call(functools.partial(kernel, (nx, ny, nz, X, Y, Z)), out_shap...  43.5 us
    unnamed x1, local copies, waits for them, and re-layouts  2.06 us

profile of v5, /device:TPU:0, one launch (start us, length us, event | category | flops | bytes accessed | tf_op | source)
XLA Modules:
  0.0 45.5 jit_solution(13617995154580202259)
XLA Ops:
  0.0 43.5 %shard_map.46 = bf16[6,512,128]{2,1,0:T(8,128)(2,1)} custom-call(s32[512,128]{1,0:T(8,128)} %bitcast.6, f32[512,128]{1,0:T(8,128)} %bitcast.7, bf16[3,512,128]{2,1,0:T(8,128)(2,1)} %bitcast.5, f32[32,16,128]{2,1,0:T(8,128)} %stiff.1), custom_call_target="tpu_custom_call" | custom-call | tf_op jit(solution)/shard_map/pallas_call | solution.py:369
  43.5 2.1 %copy.6 = bf16[6,64,8,128]{3,2,1,0:T(8,128)(2,1)} copy(bf16[6,64,8,128]{3,2,1,0:T(8,128)(2,1)} %bitcast.4) | data formatting | bytes 1572864
